TPU v7x, 512 devices: a whole 4x8x8 slice. The times are simulated.
512 devices in a mesh: dp: 16 (over y, core), seq: 32 (over z, x).
Axes of the slice: x: 4, y: 8, z: 8, core: 2. Of those that a mesh axis runs over, the one named last changes fastest.
Arguments:
- queries: bfloat16 [16, 4096, 2048], P('dp', 'seq'), may hold values from -6 to 6
- keys: bfloat16 [16, 4096, 2048], P('dp', 'seq'), may hold values from -6 to 6
- values: bfloat16 [16, 4096, 2048], P('dp', 'seq'), may hold values from -6 to 6
- out_grad: bfloat16 [16, 4096, 2048], P('dp', 'seq'), may hold values from -21 to 21
- cluster_perm: int32 [16, 4096], P('dp'), may hold values from 0 to 4095, each once within a row
- tile_ids: int32 [16, 32, 8], P('dp'), may hold values from 0 to 31, as said below
- tile_counts: int32 [16, 32], P('dp'), may hold values from 1 to 8, 128 in all within a row
- hop_class: int32 [16, 32, 8], P('dp'), may hold values from 0 to 7
- hop_bias: float32 [8, 32], replicated, may hold values from -2 to 2
Outputs:
- attended: bfloat16 [16, 4096, 2048], P('dp', 'seq')
- query_grad: bfloat16 [16, 4096, 2048], P('dp', 'seq')
- key_grad: bfloat16 [16, 4096, 2048], P('dp', 'seq')
- value_grad: bfloat16 [16, 4096, 2048], P('dp', 'seq')
- bias_grad: float32 [8, 32], replicated
Inputs may be any that keep to these rules, and one draw needn't show every extreme that they name: `tile_ids`: slot 0 of query tile t holds t; the 8 slots of a query tile name distinct tiles; slots at or past the tile's count are not used.
All inputs are finite; a program needn't handle non-finite values.
Results may differ from a plain program's by a relative error of at most 0.011.
Values may be sent and summed in bfloat16 or wider, within the bound.
A program may use at most 64 MiB of HBM per device.

v0:
```python
import jax
import jax.numpy as jnp
from jax import lax
from jax.sharding import PartitionSpec as P

TILE = 128


exact_mode = lax.Precision.HIGHEST


def tile_pass(
    query_heads,
    key_heads,
    value_heads,
    grad_heads,
    tile_list,
    tile_count,
    class_list,
    bias_cols,
    backward,
):
    node_total, local_heads, head_width = query_heads.shape
    tile_total = node_total // TILE
    slot_total = tile_list.shape[-1]
    classes = bias_cols.shape[0]
    steps_total = tile_total // 4
    key_tiles = key_heads.reshape(tile_total, TILE, local_heads, head_width)
    value_tiles = value_heads.reshape(tile_total, TILE, local_heads, head_width)

    def blocked(tensor):
        return tensor.reshape((steps_total, 4) + tensor.shape[1:])

    inputs = (
        blocked(query_heads.reshape(tile_total, TILE, local_heads, head_width)),
        blocked(grad_heads.reshape(tile_total, TILE, local_heads, head_width)),
        blocked(tile_list),
        blocked(tile_count),
        blocked(class_list),
    )

    def advance(totals, inputs_now):
        query_now, grad_now, list_now, count_now, class_now = inputs_now
        key_now = key_tiles[list_now]
        value_now = value_tiles[list_now]
        class_hot = (class_now[..., None] == jnp.arange(classes)[None, None, :]).astype(jnp.float32)
        bias_now = jnp.einsum("qsc,ch->qhs", class_hot, bias_cols, precision=exact_mode)
        usable = jnp.arange(slot_total)[None, :] < count_now[:, None]
        scores = jnp.einsum(
            "qahe,qsbhe->qhasb", query_now, key_now, preferred_element_type=jnp.float32
        )
        scores = scores * 0.125 + bias_now[:, :, None, :, None]
        scores = jnp.where(usable[:, None, None, :, None], scores, -1e30)
        row_peak = jnp.max(scores, axis=(3, 4), keepdims=True)
        powers = jnp.exp(scores - row_peak)
        weights = powers / jnp.sum(powers, axis=(3, 4), keepdims=True)
        weights_low = weights.astype(jnp.bfloat16)
        attended = jnp.einsum(
            "qhasb,qsbhe->qahe", weights_low, value_now, preferred_element_type=jnp.float32
        ).astype(jnp.bfloat16)
        if not backward:
            return (totals, attended)
        prob_grad = jnp.einsum(
            "qahe,qsbhe->qhasb", grad_now, value_now, preferred_element_type=jnp.float32
        )
        row_dot = jnp.sum(weights * prob_grad, axis=(3, 4), keepdims=True)
        score_grad = weights * (prob_grad - row_dot)
        slot_sums = jnp.sum(score_grad, axis=(2, 4))
        score_low = score_grad.astype(jnp.bfloat16)
        query_grad = (
            jnp.einsum("qhasb,qsbhe->qahe", score_low, key_now, preferred_element_type=jnp.float32)
            * 0.125
        ).astype(jnp.bfloat16)
        key_part = (
            jnp.einsum(
                "qhasb,qahe->qsbhe", score_low, query_now, preferred_element_type=jnp.float32
            )
            * 0.125
        )
        value_part = jnp.einsum(
            "qhasb,qahe->qsbhe", weights_low, grad_now, preferred_element_type=jnp.float32
        )
        placing = (list_now[..., None] == jnp.arange(tile_total)[None, None, :]).astype(jnp.float32)
        key_total = totals[0] + jnp.einsum(
            "qst,qsbhe->tbhe", placing, key_part, precision=exact_mode
        )
        value_total = totals[1] + jnp.einsum(
            "qst,qsbhe->tbhe", placing, value_part, precision=exact_mode
        )
        bias_total = totals[2] + jnp.einsum(
            "qsc,qhs->ch", class_hot, slot_sums, precision=exact_mode
        )
        return ((key_total, value_total, bias_total), (attended, query_grad))

    shape_back = (node_total, local_heads, head_width)
    if not backward:
        unused, stacked = lax.scan(advance, jnp.zeros((), jnp.float32), inputs)
        return stacked.reshape(shape_back)
    start = (
        jnp.zeros((tile_total, TILE, local_heads, head_width), jnp.float32),
        jnp.zeros((tile_total, TILE, local_heads, head_width), jnp.float32),
        jnp.zeros((classes, local_heads), jnp.float32),
    )
    totals, stacked = lax.scan(advance, start, inputs)
    return (
        stacked[0].reshape(shape_back),
        stacked[1].reshape(shape_back),
        totals[0].astype(jnp.bfloat16).reshape(shape_back),
        totals[1].astype(jnp.bfloat16).reshape(shape_back),
        totals[2],
    )


def local(
    queries, keys, values, out_grad, cluster_perm, tile_ids, tile_counts, hop_class, hop_bias
):
    device_rows = queries.shape[1]
    head_total = hop_bias.shape[1]
    head_width = queries.shape[2] // head_total
    local_heads = head_total // lax.axis_size("seq")
    node_order = cluster_perm[0]
    inverse = jnp.argsort(node_order)
    bias_cols = lax.dynamic_slice_in_dim(
        hop_bias, lax.axis_index("seq") * local_heads, local_heads, 1
    )
    tile_list = tile_ids[0]
    tile_count = tile_counts[0]
    class_list = hop_class[0]

    def split_heads(tensor):
        return tensor[0].reshape(device_rows, head_total, head_width)

    def cluster(tensor):
        return tensor[node_order]

    def restore(tensor):
        return tensor[inverse]

    def join_heads(tensor):
        return tensor.reshape(1, device_rows, head_total * head_width)

    query_heads, key_heads, value_heads = (
        lax.all_to_all(split_heads(queries), "seq", split_axis=1, concat_axis=0, tiled=True),
        lax.all_to_all(split_heads(keys), "seq", split_axis=1, concat_axis=0, tiled=True),
        lax.all_to_all(split_heads(values), "seq", split_axis=1, concat_axis=0, tiled=True),
    )
    query_heads = cluster(query_heads)
    key_heads = cluster(key_heads)
    value_heads = cluster(value_heads)
    attended = tile_pass(
        query_heads,
        key_heads,
        value_heads,
        query_heads,
        tile_list,
        tile_count,
        class_list,
        bias_cols,
        False,
    )
    attended = lax.all_to_all(restore(attended), "seq", split_axis=0, concat_axis=1, tiled=True)
    grad_heads = cluster(
        lax.all_to_all(split_heads(out_grad), "seq", split_axis=1, concat_axis=0, tiled=True)
    )
    recomputed, query_grad, key_grad, value_grad, bias_part = tile_pass(
        query_heads,
        key_heads,
        value_heads,
        grad_heads,
        tile_list,
        tile_count,
        class_list,
        bias_cols,
        True,
    )
    query_grad, key_grad, value_grad = (
        lax.all_to_all(restore(query_grad), "seq", split_axis=0, concat_axis=1, tiled=True),
        lax.all_to_all(restore(key_grad), "seq", split_axis=0, concat_axis=1, tiled=True),
        lax.all_to_all(restore(value_grad), "seq", split_axis=0, concat_axis=1, tiled=True),
    )
    padded = jnp.zeros((bias_part.shape[0], head_total), jnp.float32)
    padded = lax.dynamic_update_slice_in_dim(
        padded, bias_part, lax.axis_index("seq") * local_heads, 1
    )
    bias_grad = lax.psum(padded, ("dp", "seq"))
    return (
        join_heads(attended),
        join_heads(query_grad),
        join_heads(key_grad),
        join_heads(value_grad),
        bias_grad,
    )


def solution(mesh):
    return jax.shard_map(
        local,
        mesh=mesh,
        in_specs=(
            P("dp", "seq", None),
            P("dp", "seq", None),
            P("dp", "seq", None),
            P("dp", "seq", None),
            P("dp", None),
            P("dp", None, None),
            P("dp", None),
            P("dp", None, None),
            P(),
        ),
        out_specs=(
            P("dp", "seq", None),
            P("dp", "seq", None),
            P("dp", "seq", None),
            P("dp", "seq", None),
            P(),
        ),
        check_vma=False,
    )
```

profile of v0, /device:TPU:1, one launch (start us, length us, event | category | flops | bytes accessed | tf_op | source)
XLA Modules:
  0.0 579.1 jit_solution(16644537729558474420)
XLA Ops:
  0.7 2.1 copy.129
  2.8 13.7 %all-to-all-start = ((bf16[128,32,64]{0,2,1:T(8,128)(2,1)}), bf16[128,32,64]{0,2,1:T(8,128)(2,1)S(1)}, u32[]{:S(2)}, u32[]{:S(2)}) async-start(bf16[128,32,64]{0,2,1:T(8,128)(2,1)} %bitcast.20), calls=%async_computation | async-start | bytes 1048576 | tf_op jit(solution)/shard_map/all_to_all | solution.py:145
  17.5 15.3 %all-to-all-done = bf16[128,32,64]{0,2,1:T(8,128)(2,1)S(1)} async-done(((bf16[128,32,64]{0,2,1:T(8,128)(2,1)}), bf16[128,32,64]{0,2,1:T(8,128)(2,1)S(1)}, u32[]{:S(2)}, u32[]{:S(2)}) %all-to-all-start) | async-done | bytes 524320 | tf_op jit(solution)/shard_map/all_to_all | solution.py:145
  32.8 5.4 all-to-all-start.1
  39.2 14.0 %all-to-all-done.1 = bf16[128,32,64]{0,2,1:T(8,128)(2,1)S(1)} async-done(((bf16[128,32,64]{0,2,1:T(8,128)(2,1)}), bf16[128,32,64]{0,2,1:T(8,128)(2,1)S(1)}, u32[]{:S(2)}, u32[]{:S(2)}) %all-to-all-start.1) | async-done | bytes 524320 | tf_op jit(solution)/shard_map/all_to_all | solution.py:143
  53.2 6.4 %all-to-all-start.2 = ((bf16[128,32,64]{0,2,1:T(8,128)(2,1)}), bf16[128,32,64]{0,2,1:T(8,128)(2,1)S(1)}, u32[]{:S(2)}, u32[]{:S(2)}) async-start(bf16[128,32,64]{0,2,1:T(8,128)(2,1)} %bitcast.32), calls=%async_computation.2 | async-start | bytes 1048576 | tf_op jit(solution)/shard_map/all_to_all | solution.py:144
  62.2 5.8 sort.17
  68.0 6.6 %all-to-all-done.2 = bf16[128,32,64]{0,2,1:T(8,128)(2,1)S(1)} async-done(((bf16[128,32,64]{0,2,1:T(8,128)(2,1)}), bf16[128,32,64]{0,2,1:T(8,128)(2,1)S(1)}, u32[]{:S(2)}, u32[]{:S(2)}) %all-to-all-start.2) | async-done | bytes 524320 | tf_op jit(solution)/shard_map/all_to_all | solution.py:144
  74.6 6.7 %all-to-all-start.4 = ((bf16[128,32,64]{0,2,1:T(8,128)(2,1)}), bf16[128,32,64]{0,2,1:T(8,128)(2,1)}, u32[]{:S(2)}, u32[]{:S(2)}) async-start(bf16[128,32,64]{0,2,1:T(8,128)(2,1)} %bitcast.43), calls=%async_computation.4 | async-start | bytes 1048576 | tf_op jit(solution)/shard_map/all_to_all | solution.py:163
  81.8 12.1 %gather_fusion.4 = bf16[4096,64]{1,0:T(8,128)(2,1)S(1)} fusion(bf16[4096,64]{1,0:T(8,128)(2,1)S(1)} %bitcast.320, s32[4096]{0:T(1024)S(1)} %broadcast_clamp_fusion), kind=kCustom, calls=%fused_computation.4 | custom fusion | bytes 1064960 | tf_op jit(solution)/shard_map/gather | solution.py:134
  94.9 12.1 %gather_fusion.5 = bf16[4096,64]{1,0:T(8,128)(2,1)S(1)} fusion(bf16[4096,64]{1,0:T(8,128)(2,1)S(1)} %bitcast.321, s32[4096]{0:T(1024)S(1)} %broadcast_clamp_fusion), kind=kCustom, calls=%fused_computation.5 | custom fusion | bytes 1064960 | tf_op jit(solution)/shard_map/gather | solution.py:134
  108.7 12.1 %gather_fusion.6 = bf16[4096,64]{1,0:T(8,128)(2,1)S(1)} fusion(bf16[4096,64]{1,0:T(8,128)(2,1)S(1)} %bitcast.322, s32[4096]{0:T(1024)S(1)} %broadcast_clamp_fusion), kind=kCustom, calls=%fused_computation.6 | custom fusion | bytes 1064960 | tf_op jit(solution)/shard_map/gather | solution.py:134
  122.8 12.1 %gather_fusion.8 = bf16[4096,64]{1,0:T(8,128)(2,1)S(1)} fusion(bf16[4096,64]{1,0:T(8,128)(2,1)S(1)} %bitcast.318, s32[4096]{0:T(1024)S(1)} %broadcast_clamp_fusion), kind=kCustom, calls=%fused_computation.8 | custom fusion | bytes 1064960 | tf_op jit(solution)/shard_map/gather | solution.py:134
  137.0 148.7 %while.28 = (s32[]{:T(128)}, f32[32,128,1,64]{1,0,3,2:T(8,128)}, f32[32,128,1,64]{1,0,3,2:T(8,128)}, f32[8,1]{0,1:T(1,128)S(1)}, bf16[8,4,128,1,64]{2,4,1,3,0:T(...) while((s32[]{:T(128)}, f32[32,128,1,64]{1,0,3,2:T(8,128)}, ...), condition=%wide.region_10.11_spmd.clone, body=%wide.region_5.10_spmd.clone.sunk | while | flops 548216960 | bytes 40729924 | solution.py:104
  140.9 2.4 convolution_bitcast_fusion.7
  143.3 3.5 fusion.122
  148.2 1.8 multiply_reduce_fusion.2
  159.3 2.4 convolution_bitcast_fusion.7
  161.6 3.8 fusion.122
  166.9 1.8 multiply_reduce_fusion.2
  177.9 2.4 convolution_bitcast_fusion.7
  180.3 3.8 fusion.122
  185.5 1.8 multiply_reduce_fusion.2
  196.5 2.4 convolution_bitcast_fusion.7
  198.9 3.8 fusion.122
  204.1 1.8 multiply_reduce_fusion.2
  215.2 2.4 convolution_bitcast_fusion.7
  217.5 3.8 fusion.122
  222.8 1.8 multiply_reduce_fusion.2
  233.8 2.4 convolution_bitcast_fusion.7
  236.1 3.8 fusion.122
  241.4 1.8 multiply_reduce_fusion.2
  252.4 2.4 convolution_bitcast_fusion.7
  254.8 3.8 fusion.122
  260.0 1.8 multiply_reduce_fusion.2
  271.0 2.4 convolution_bitcast_fusion.7
  273.4 3.8 fusion.122
  278.6 1.8 multiply_reduce_fusion.2
  287.7 12.1 %gather_fusion.10 = bf16[4096,64]{1,0:T(8,128)(2,1)S(1)} fusion(bf16[4096,64]{1,0:T(8,128)(2,1)S(1)} %bitcast.323, s32[4096]{0:T(1024)S(1)} %fusion.50), kind=kCustom, calls=%fused_computation.10 | custom fusion | bytes 1064960 | tf_op jit(solution)/shard_map/gather | solution.py:137
  300.3 2.2 reduce.18
  302.5 3.0 reshape.508
  305.6 9.1 %all-to-all-start.6 = ((bf16[32,2,4096]{2,1,0:T(2,128)(2,1)}), bf16[32,2,4096]{2,1,0:T(2,128)(2,1)}, u32[]{:S(2)}, u32[]{:S(2)}) async-start(bf16[32,2,4096]{2,1,0:T(2,128)(2,1)} %reshape.508), calls=%async_computation.6 | async-start | bytes 1048576 | tf_op jit(solution)/shard_map/all_to_all | solution.py:178
  315.5 12.1 %gather_fusion.11 = bf16[4096,64]{1,0:T(8,128)(2,1)S(1)} fusion(bf16[4096,64]{1,0:T(8,128)(2,1)S(1)} %bitcast.324, s32[4096]{0:T(1024)S(1)} %fusion.50), kind=kCustom, calls=%fused_computation.11 | custom fusion | bytes 1064960 | tf_op jit(solution)/shard_map/gather | solution.py:137
  330.8 9.3 %all-to-all-start.7 = ((bf16[32,2,4096]{2,1,0:T(2,128)(2,1)}), bf16[32,2,4096]{2,1,0:T(2,128)(2,1)}, u32[]{:S(2)}, u32[]{:S(2)}) async-start(bf16[32,2,4096]{2,1,0:T(2,128)(2,1)} %reshape.510), calls=%async_computation.7 | async-start | bytes 1048576 | tf_op jit(solution)/shard_map/all_to_all | solution.py:179
  340.6 12.1 %gather_fusion.9 = bf16[4096,64]{1,0:T(8,128)(2,1)S(1)} fusion(bf16[4096,64]{1,0:T(8,128)(2,1)S(1)} %bitcast.325, s32[4096]{0:T(1024)S(1)} %fusion.50), kind=kCustom, calls=%fused_computation.9 | custom fusion | bytes 1064960 | tf_op jit(solution)/shard_map/gather | solution.py:137
  355.9 9.1 %all-to-all-start.5 = ((bf16[32,2,4096]{2,1,0:T(2,128)(2,1)}), bf16[32,2,4096]{2,1,0:T(2,128)(2,1)S(1)}, u32[]{:S(2)}, u32[]{:S(2)}) async-start(bf16[32,2,4096]{2,1,0:T(2,128)(2,1)} %reshape.506), calls=%async_computation.5 | async-start | bytes 1048576 | tf_op jit(solution)/shard_map/all_to_all | solution.py:177
  365.1 55.1 %while.27 = (s32[]{:T(128)}, bf16[8,4,128,1,64]{2,4,1,3,0:T(8,128)(2,1)S(1)}, s32[8,4,8]{2,1,0:T(4,128)S(1)}, bf16[32,128,1,64]{1,3,2,0:T(8,128)(2,1)S(1)}, s32[...) while((s32[]{:T(128)}, ...), condition=%wide.region_3.4_spmd, body=%wide.region_0.3_spmd.sunk | while | flops 138972544 | bytes 17973536 | solution.py:97
  369.9 2.2 fusion.100
  376.8 2.2 fusion.100
  383.6 2.2 fusion.100
  390.5 2.2 fusion.100
  397.4 2.2 fusion.100
  404.3 2.2 fusion.100
  411.2 2.2 fusion.100
  418.1 2.2 fusion.100
  420.8 12.1 %gather_fusion.7 = bf16[4096,64]{1,0:T(8,128)(2,1)S(1)} fusion(bf16[4096,64]{1,0:T(8,128)(2,1)S(1)} %bitcast.319, s32[4096]{0:T(1024)S(1)} %fusion.50), kind=kCustom, calls=%fused_computation.7 | custom fusion | bytes 1064960 | tf_op jit(solution)/shard_map/gather | solution.py:137
  436.1 9.2 %all-to-all-start.3 = ((bf16[32,2,4096]{2,1,0:T(2,128)(2,1)}), bf16[32,2,4096]{2,1,0:T(2,128)(2,1)S(1)}, u32[]{:S(2)}, u32[]{:S(2)}) async-start(bf16[32,2,4096]{2,1,0:T(2,128)(2,1)} %reshape.504), calls=%async_computation.3 | async-start | bytes 1048576 | tf_op jit(solution)/shard_map/all_to_all | solution.py:161
  445.7 103.4 %psum.7 = f32[8,32]{1,0:T(8,128)} all-reduce(f32[8,32]{1,0:T(8,128)S(1)} %dynamic_update_slice.10), channel_id=1, replica_groups=mesh['dp'=16,'seq'=32] {'dp','seq'}, use_global_device_ids=true, to_apply=%region_11.12 | all-reduce | flops 256 | bytes 2048 | tf_op jit(solution)/shard_map/psum | solution.py:185
  549.1 4.1 reshape.509
  553.2 3.6 copy.156
  559.2 4.1 reshape.511
  563.4 3.6 copy.160
  570.6 2.3 copy.152
  575.4 2.3 copy.142
  (362 shorter events, 157.6 us)
Async XLA Ops:
  0.6 59.0 %copy-start = (f32[8,32]{1,0:T(8,128)S(1)}, f32[8,32]{1,0:T(8,128)}, u32[]{:S(2)}) copy-start(f32[8,32]{1,0:T(8,128)} %param.21) | copy-start | bytes 3076
  0.6 15.9 %copy-start.7 = (bf16[1,128,2048]{2,1,0:T(8,128)(2,1)S(1)}, bf16[1,128,2048]{2,1,0:T(8,128)(2,1)}, u32[]{:S(2)}) copy-start(bf16[1,128,2048]{2,1,0:T(8,128)(2,1)} %param.13) | copy-start | bytes 1572868
  0.7 37.5 %copy-start.8 = (bf16[1,128,2048]{2,1,0:T(8,128)(2,1)S(1)}, bf16[1,128,2048]{2,1,0:T(8,128)(2,1)}, u32[]{:S(2)}) copy-start(bf16[1,128,2048]{2,1,0:T(8,128)(2,1)} %param.14) | copy-start | bytes 1572868
  2.8 30.0 %all-to-all-start = ((bf16[128,32,64]{0,2,1:T(8,128)(2,1)}), bf16[128,32,64]{0,2,1:T(8,128)(2,1)S(1)}, u32[]{:S(2)}, u32[]{:S(2)}) async-start(bf16[128,32,64]{0,2,1:T(8,128)(2,1)} %bitcast.20), calls=%async_computation | async-start | bytes 1048576 | tf_op jit(solution)/shard_map/all_to_all | solution.py:145
  16.5 43.3 %copy-start.9 = (bf16[1,128,2048]{2,1,0:T(8,128)(2,1)S(1)}, bf16[1,128,2048]{2,1,0:T(8,128)(2,1)}, u32[]{:S(2)}) copy-start(bf16[1,128,2048]{2,1,0:T(8,128)(2,1)} %param.16) | copy-start | bytes 1572868
  32.8 28.0 %copy-start.11 = (s32[1,32,8]{1,2,0:T(8,128)S(1)}, s32[1,32,8]{1,2,0:T(8,128)}, u32[]{:S(2)}) copy-start(s32[1,32,8]{1,2,0:T(8,128)} %param.18) | copy-start | bytes 3076
  32.8 28.1 %copy-start.12 = (s32[1,32,8]{1,2,0:T(8,128)S(1)}, s32[1,32,8]{1,2,0:T(8,128)}, u32[]{:S(2)}) copy-start(s32[1,32,8]{1,2,0:T(8,128)} %param.20) | copy-start | bytes 3076
  32.8 28.7 %copy-start.13 = (s32[1,32]{1,0:T(1,128)S(1)}, s32[1,32]{1,0:T(1,128)}, u32[]{:S(2)}) copy-start(s32[1,32]{1,0:T(1,128)} %param.19) | copy-start | bytes 388
  32.8 29.4 %copy-start.10 = (s32[1,4096]{1,0:T(1,128)S(1)}, s32[1,4096]{1,0:T(1,128)}, u32[]{:S(2)}) copy-start(s32[1,4096]{1,0:T(1,128)} %param.17) | copy-start | bytes 49156
  32.8 20.4 %all-to-all-start.1 = ((bf16[128,32,64]{0,2,1:T(8,128)(2,1)}), bf16[128,32,64]{0,2,1:T(8,128)(2,1)S(1)}, u32[]{:S(2)}, u32[]{:S(2)}) async-start(bf16[128,32,64]{0,2,1:T(8,128)(2,1)} %bitcast.27), calls=%async_computation.1 | async-start | bytes 1048576 | tf_op jit(solution)/shard_map/all_to_all | solution.py:143
  53.2 21.4 %all-to-all-start.2 = ((bf16[128,32,64]{0,2,1:T(8,128)(2,1)}), bf16[128,32,64]{0,2,1:T(8,128)(2,1)S(1)}, u32[]{:S(2)}, u32[]{:S(2)}) async-start(bf16[128,32,64]{0,2,1:T(8,128)(2,1)} %bitcast.32), calls=%async_computation.2 | async-start | bytes 1048576 | tf_op jit(solution)/shard_map/all_to_all | solution.py:144
  74.6 46.6 %all-to-all-start.4 = ((bf16[128,32,64]{0,2,1:T(8,128)(2,1)}), bf16[128,32,64]{0,2,1:T(8,128)(2,1)}, u32[]{:S(2)}, u32[]{:S(2)}) async-start(bf16[128,32,64]{0,2,1:T(8,128)(2,1)} %bitcast.43), calls=%async_computation.4 | async-start | bytes 1048576 | tf_op jit(solution)/shard_map/all_to_all | solution.py:163
  150.9 1.4 copy-start.3
  152.3 1.7 copy-start.1
  154.0 1.2 copy-start.4
  169.5 1.4 copy-start.3
  171.0 1.7 copy-start.1
  172.7 1.2 copy-start.4
  188.2 1.4 copy-start.3
  189.6 1.7 copy-start.1
  191.3 1.2 copy-start.4
  206.8 1.4 copy-start.3
  208.2 1.7 copy-start.1
  209.9 1.2 copy-start.4
  225.4 1.4 copy-start.3
  226.9 1.7 copy-start.1
  228.6 1.2 copy-start.4
  244.1 1.4 copy-start.3
  245.5 1.7 copy-start.1
  247.2 1.2 copy-start.4
  262.7 1.4 copy-start.3
  264.1 1.7 copy-start.1
  265.8 1.2 copy-start.4
  281.3 1.4 copy-start.3
  282.7 1.7 copy-start.1
  284.5 1.2 copy-start.4
  300.3 14.4 %copy-start.5 = (f32[32,128,1,64]{1,0,3,2:T(8,128)S(1)}, f32[32,128,1,64]{1,0,3,2:T(8,128)}, u32[]{:S(2)}) copy-start(f32[32,128,1,64]{1,0,3,2:T(8,128)} %get-tuple-element.127) | copy-start | bytes 3145732
  305.6 25.2 %all-to-all-start.6 = ((bf16[32,2,4096]{2,1,0:T(2,128)(2,1)}), bf16[32,2,4096]{2,1,0:T(2,128)(2,1)}, u32[]{:S(2)}, u32[]{:S(2)}) async-start(bf16[32,2,4096]{2,1,0:T(2,128)(2,1)} %reshape.508), calls=%async_computation.6 | async-start | bytes 1048576 | tf_op jit(solution)/shard_map/all_to_all | solution.py:178
  329.2 10.8 %copy-start.6 = (bf16[8,4,128,1,64]{2,4,1,3,0:T(8,128)(2,1)S(1)}, bf16[8,4,128,1,64]{2,4,1,3,0:T(8,128)(2,1)}, u32[]{:S(2)}) copy-start(bf16[8,4,128,1,64]{2,4,1,3,0:T(8,128)(2,1)} %get-tuple-element.125) | copy-start | bytes 1572868
  330.8 25.1 %all-to-all-start.7 = ((bf16[32,2,4096]{2,1,0:T(2,128)(2,1)}), bf16[32,2,4096]{2,1,0:T(2,128)(2,1)}, u32[]{:S(2)}, u32[]{:S(2)}) async-start(bf16[32,2,4096]{2,1,0:T(2,128)(2,1)} %reshape.510), calls=%async_computation.7 | async-start | bytes 1048576 | tf_op jit(solution)/shard_map/all_to_all | solution.py:179
  355.9 80.2 %all-to-all-start.5 = ((bf16[32,2,4096]{2,1,0:T(2,128)(2,1)}), bf16[32,2,4096]{2,1,0:T(2,128)(2,1)S(1)}, u32[]{:S(2)}, u32[]{:S(2)}) async-start(bf16[32,2,4096]{2,1,0:T(2,128)(2,1)} %reshape.506), calls=%async_computation.5 | async-start | bytes 1048576 | tf_op jit(solution)/shard_map/all_to_all | solution.py:177
  367.8 1.4 copy-start.2
  374.7 1.4 copy-start.2
  381.6 1.4 copy-start.2
  388.5 1.4 copy-start.2
  395.4 1.4 copy-start.2
  402.3 1.4 copy-start.2
  409.2 1.4 copy-start.2
  416.1 1.4 copy-start.2
  436.1 138.1 %all-to-all-start.3 = ((bf16[32,2,4096]{2,1,0:T(2,128)(2,1)}), bf16[32,2,4096]{2,1,0:T(2,128)(2,1)S(1)}, u32[]{:S(2)}, u32[]{:S(2)}) async-start(bf16[32,2,4096]{2,1,0:T(2,128)(2,1)} %reshape.504), calls=%async_computation.3 | async-start | bytes 1048576 | tf_op jit(solution)/shard_map/all_to_all | solution.py:161
where the time goes:
time: 582 us; the launch traced here: 579 us
  local copies, waits for them, and re-layouts  194 us (33%)
  matrix products  146 us (25%)
  blocking collectives  103 us (18%)
  starting transfers between devices  68.8 us (12%)
  waiting for transfers between devices  35.9 us (6%)
  other arithmetic  28.1 us (5%)
    psum x1, blocking collectives, local(): bias_grad = lax.psum(padded, ('dp', 'seq'))  103 us
    gather x5, local copies, waits for them, and re-layouts, restore(): return tensor[inverse]  49 us
    gather x4, local copies, waits for them, and re-layouts, cluster(): return tensor[node_order]  48.5 us
    unnamed x45, local copies, waits for them, and re-layouts  32 us
    dot_general x8, matrix products, advance(): jnp.einsum('qst,qsbhe->tbhe', placing, value_part, precision=exact_mode)  30.4 us
    dot_general x16, matrix products, advance(): jnp.einsum('qahe,qsbhe->qhasb', query_now, key_now, preferred_element_typ...  26.6 us
    dot_general x8, matrix products, advance(): jnp.einsum('qhasb,qahe->qsbhe', weights_low, grad_now, preferred_element_...  18.9 us
    dot_general x8, matrix products, advance(): jnp.einsum('qhasb,qsbhe->qahe', weights_low, value_now, preferred_element...  17.2 us
  transfers between devices with their start and end apart: 8, of which 3 were waited for; matrix products, arithmetic and copies ran while one was open for 29% of the time, Pallas kernels for 0%

commit v1 on v0

v1 whole, which is shorter than its diff:
```python
import functools
import math

import jax
import jax.numpy as jnp
from jax import lax
from jax.experimental import pallas as pl
from jax.experimental.pallas import tpu as pltpu
from jax.sharding import PartitionSpec as P

MESH = pl.DeviceIdType.MESH
TILE = 128
LOG2E = math.log2(math.e)
NT_DIMS = (((1,), (1,)), ((), ()))


def lanes_low(shape):
    return lax.broadcasted_iota(jnp.int32, shape, len(shape) - 1) < 64


def greet(me, count):
    dp = lax.axis_index("dp")
    barrier = pltpu.get_barrier_semaphore()

    @pl.loop(1, count)
    def _(step):
        other = lax.rem(me + step, count)
        pl.semaphore_signal(barrier, inc=1, device_id=(dp, other), device_id_type=MESH)

    return barrier


def remote(src, dst, send_sem, recv_sem, other):
    return pltpu.make_async_remote_copy(
        src_ref=src,
        dst_ref=dst,
        send_sem=send_sem,
        recv_sem=recv_sem,
        device_id=(lax.axis_index("dp"), other),
        device_id_type=MESH,
    )


def rolled(block):
    return pltpu.roll(block.astype(jnp.float32), 64, 1).astype(jnp.bfloat16)


def gather_rows(source, rows_out, base, index_of):
    for r in range(TILE):
        rows_out[pl.ds(r, 1), :] = source[pl.ds(index_of(base, r), 1), :]


def inbound_kernel(
    count,
    q_ref,
    k_ref,
    v_ref,
    g_ref,
    perm_ref,
    perm_row_ref,
    ids_ref,
    counts_ref,
    class_ref,
    kv_ref,
    kvt_ref,
    qg_ref,
    inverse_ref,
    pairs_ref,
    send_kv,
    send_qg,
    recv_kv,
    wide,
    rows,
    send_sem,
    recv_sem,
):
    me = lax.axis_index("seq")
    barrier = greet(me, count)
    low = lanes_low((TILE, TILE))

    def pack(first_ref, second_ref, out):
        @pl.loop(0, count // 2)
        def _(pair):
            columns = pl.ds(pl.multiple_of(pair * TILE, TILE), TILE)
            first, second = first_ref[:, columns], second_ref[:, columns]
            out[2 * pair] = jnp.where(low, first, rolled(second))
            out[2 * pair + 1] = jnp.where(low, rolled(first), second)

    def send_all(out, landing, which):
        @pl.loop(1, count)
        def _(step):
            other = lax.rem(me + step, count)
            remote(
                out.at[other], landing.at[me], send_sem.at[which], recv_sem.at[which], other
            ).start()

        landing[me] = out[me]

    def wait_all(out, landing, which, receive):
        many = remote(
            out.at[pl.ds(0, count - 1)],
            landing.at[pl.ds(0, count - 1)],
            send_sem.at[which],
            recv_sem.at[which],
            lax.rem(me + 1, count),
        )
        if receive:
            many.wait_recv()
        else:
            many.wait_send()

    pack(k_ref, v_ref, send_kv)
    pl.semaphore_wait(barrier, count - 1)
    send_all(send_kv, recv_kv, 0)
    pack(q_ref, g_ref, send_qg)
    send_all(send_qg, qg_ref, 1)

    def list_pair(p, state):
        t, s = state
        pairs_ref[0, p] = t
        pairs_ref[1, p] = ids_ref[0, t, s]
        pairs_ref[2, p] = class_ref[0, t, s]
        more = s + 1 < counts_ref[0, t]
        following = jnp.minimum(t + 1, counts_ref.shape[1] - 1)
        return jnp.where(more, t, following), jnp.where(more, s + 1, 0)

    lax.fori_loop(0, TILE, list_pair, (jnp.int32(0), jnp.int32(0)))

    high_total = jnp.zeros((64, 64), jnp.float32)
    low_total = jnp.zeros((64, 64), jnp.float32)
    width = 1024
    nodes = perm_row_ref.shape[1]
    for start in range(0, nodes, width):
        node = perm_row_ref[:, pl.ds(start, width)]
        digit = lax.broadcasted_iota(jnp.int32, (64, width), 0)
        position = lax.broadcasted_iota(jnp.int32, (64, width), 1) + start
        at_high = lax.shift_right_logical(node, 6) == digit
        at_low = jnp.where((node & 63) == digit, 1.0, 0.0).astype(jnp.bfloat16)
        high_value = lax.shift_right_logical(position, 6).astype(jnp.float32)
        low_value = (position & 63).astype(jnp.float32)
        high_rows = jnp.where(at_high, high_value, 0.0).astype(jnp.bfloat16)
        low_rows = jnp.where(at_high, low_value, 0.0).astype(jnp.bfloat16)
        high_total += lax.dot_general(high_rows, at_low, NT_DIMS, preferred_element_type=jnp.float32)
        low_total += lax.dot_general(low_rows, at_low, NT_DIMS, preferred_element_type=jnp.float32)
    inverse_ref[...] = (high_total * 64.0 + low_total).astype(jnp.int32)

    wait_all(send_kv, recv_kv, 0, True)

    @pl.loop(0, count)
    def _(block):
        wide[pl.ds(pl.multiple_of(block * TILE, TILE), TILE), :] = recv_kv[block].astype(jnp.float32)

    @pl.loop(0, count)
    def _(tile):
        gather_rows(wide, rows, tile * TILE, lambda base, r: perm_ref[0, base + r])
        block = rows[...]
        kv_ref[tile] = block.astype(jnp.bfloat16)
        kvt_ref[tile] = block.T.astype(jnp.bfloat16)

    wait_all(send_qg, qg_ref, 1, True)
    wait_all(send_kv, recv_kv, 0, False)
    wait_all(send_qg, qg_ref, 1, False)


def attention_kernel(
    unroll,
    kv_ref,
    kvt_ref,
    qg_ref,
    perm_ref,
    pairs_ref,
    bias_ref,
    oq_ref,
    dkv_ref,
    bias_out_ref,
    wide,
    rows,
    weight,
    scores,
    grads,
    peak,
    total,
    dots,
    dkv_acc,
    oq_acc,
    bias_acc,
):
    head = lax.axis_index("seq")
    tiles = kv_ref.shape[0]
    low = lanes_low((TILE, TILE))

    @pl.loop(0, tiles)
    def _(block):
        wide[pl.ds(pl.multiple_of(block * TILE, TILE), TILE), :] = qg_ref[block].astype(jnp.float32)

    @pl.loop(0, tiles)
    def _(tile):
        gather_rows(wide, rows, tile * TILE, lambda base, r: perm_ref[0, base + r])
        block = rows[...]
        weight[tile, pl.ds(0, TILE), :] = jnp.where(low, block * 0.125, 0.0).astype(jnp.bfloat16)
        weight[tile, pl.ds(TILE, TILE), :] = jnp.where(low, 0.0, block).astype(jnp.bfloat16)

    peak[...] = jnp.full(peak.shape, -jnp.inf, jnp.float32)
    total[...] = jnp.zeros(total.shape, jnp.float32)
    dots[...] = jnp.zeros(dots.shape, jnp.float32)
    dkv_acc[...] = jnp.zeros(dkv_acc.shape, jnp.float32)
    oq_acc[...] = jnp.zeros(oq_acc.shape, jnp.float32)
    bias_acc[...] = jnp.zeros(bias_acc.shape, jnp.float32)

    def folded(block):
        return block.reshape(TILE // 8, 8, TILE)

    @pl.loop(0, TILE // unroll)
    def _(step):
        for u in range(unroll):
            p = step * unroll + u
            t, j = pairs_ref[0, p], pairs_ref[1, p]
            bias = bias_ref[pairs_ref[2, p], head] * LOG2E
            both = lax.dot_general(kv_ref[j], weight[t], NT_DIMS, preferred_element_type=jnp.float32)
            score = both[:, :TILE] * LOG2E + bias
            scores[p] = score
            grads[p] = both[:, TILE:]
            peak[t] = jnp.maximum(peak[t], jnp.max(folded(score), axis=0))

    peak[...] = jnp.broadcast_to(jnp.max(peak[...], axis=1, keepdims=True), peak.shape)

    @pl.loop(0, TILE // unroll)
    def _(step):
        for u in range(unroll):
            p = step * unroll + u
            t = pairs_ref[0, p]
            power = jnp.exp2(folded(scores[p]) - peak[t][None])
            scores[p] = power.reshape(TILE, TILE)
            total[t] = total[t] + jnp.sum(power, axis=0)
            dots[t] = dots[t] + jnp.sum(power * folded(grads[p]), axis=0)

    scale = 1.0 / jnp.sum(total[...], axis=1, keepdims=True)
    delta = jnp.sum(dots[...], axis=1, keepdims=True) * scale
    total[...] = jnp.broadcast_to(scale, total.shape)
    dots[...] = jnp.broadcast_to(delta, dots.shape)

    @pl.loop(0, TILE // unroll)
    def _(step):
        for u in range(unroll):
            p = step * unroll + u
            t, j, c = pairs_ref[0, p], pairs_ref[1, p], pairs_ref[2, p]
            prob = folded(scores[p]) * total[t][None]
            score_grad = prob * (folded(grads[p]) - dots[t][None])
            bias_acc[c] = bias_acc[c] + jnp.sum(score_grad, axis=0)
            prob_low = prob.reshape(TILE, TILE).astype(jnp.bfloat16)
            grad_low = score_grad.reshape(TILE, TILE).astype(jnp.bfloat16)
            dkv_acc[j] = dkv_acc[j] + jnp.dot(
                jnp.concatenate([grad_low, prob_low], axis=1),
                weight[t],
                preferred_element_type=jnp.float32,
            )
            kvt = kvt_ref[j]
            oq_acc[t, pl.ds(0, 64), :] = oq_acc[t, pl.ds(0, 64), :] + jnp.dot(
                kvt[:64], grad_low, preferred_element_type=jnp.float32
            )
            oq_acc[t, pl.ds(64, 64), :] = oq_acc[t, pl.ds(64, 64), :] + jnp.dot(
                kvt[64:], prob_low, preferred_element_type=jnp.float32
            )

    @pl.loop(0, tiles)
    def _(tile):
        block = oq_acc[tile].T
        oq_ref[tile] = jnp.where(low, block * 0.125, block)
        dkv_ref[tile] = dkv_acc[tile]

    class_sums = jnp.sum(jnp.sum(bias_acc[...], axis=1), axis=1, keepdims=True)
    column = lax.broadcasted_iota(jnp.int32, bias_out_ref.shape, 1)
    bias_out_ref[...] = jnp.where(column == head, class_sums, 0.0)


def outbound_kernel(
    count,
    oq_ref,
    dkv_ref,
    inverse_ref,
    bias_ref,
    o_ref,
    dq_ref,
    dk_ref,
    dv_ref,
    bias_out_ref,
    send_oq,
    send_dkv,
    recv_oq,
    recv_dkv,
    rows,
    bias_groups,
    bias_sum,
    bias_heads,
    send_sem,
    recv_sem,
):
    me = lax.axis_index("seq")
    group, groups = lax.axis_index("dp"), bias_groups.shape[0]
    barrier = greet(me, count)

    @pl.loop(1, groups)
    def _(step):
        other = lax.rem(group + step, groups)
        pl.semaphore_signal(barrier, inc=1, device_id=(other, me), device_id_type=MESH)

    low = lanes_low((TILE, TILE))
    pl.semaphore_wait(barrier, count + groups - 2)

    def bias_to_group(step):
        other = lax.rem(group + step, groups)
        return pltpu.make_async_remote_copy(
            src_ref=bias_ref,
            dst_ref=bias_groups.at[group],
            send_sem=send_sem.at[2],
            recv_sem=recv_sem.at[2],
            device_id=(other, me),
            device_id_type=MESH,
        )

    @pl.loop(1, groups)
    def _(step):
        bias_to_group(step).start()

    bias_groups[group] = bias_ref[...]

    def send_all(source, out, landing, which):
        def fill(other):
            gather_rows(
                source,
                rows,
                other,
                lambda base, r: inverse_ref[2 * base + r // 64, r % 64],
            )
            return rows[...].astype(jnp.bfloat16)

        @pl.loop(1, count)
        def _(step):
            other = lax.rem(me + step, count)
            out[other] = fill(other)
            remote(
                out.at[other], landing.at[me], send_sem.at[which], recv_sem.at[which], other
            ).start()

        landing[me] = fill(me)

    def wait_all(out, landing, which, receive, parties=count):
        many = remote(
            out.at[pl.ds(0, parties - 1)],
            landing.at[pl.ds(0, parties - 1)],
            send_sem.at[which],
            recv_sem.at[which],
            lax.rem(me + 1, count),
        )
        if receive:
            many.wait_recv()
        else:
            many.wait_send()

    def unpack(landing, first_ref, second_ref):
        @pl.loop(0, count // 2)
        def _(pair):
            columns = pl.ds(pl.multiple_of(pair * TILE, TILE), TILE)
            even, odd = landing[2 * pair], landing[2 * pair + 1]
            first_ref[:, columns] = jnp.where(low, even, rolled(odd))
            second_ref[:, columns] = jnp.where(low, rolled(even), odd)

    send_all(oq_ref, send_oq, recv_oq, 0)
    wait_all(bias_groups, bias_groups, 2, True, groups)
    bias_sum[...] = jnp.sum(bias_groups[...], axis=0)

    @pl.loop(1, count)
    def _(step):
        other = lax.rem(me + step, count)
        remote(bias_sum, bias_heads.at[me], send_sem.at[3], recv_sem.at[3], other).start()

    bias_heads[me] = bias_sum[...]
    send_all(dkv_ref, send_dkv, recv_dkv, 1)
    wait_all(bias_heads, bias_heads, 3, True)
    bias_out_ref[...] = jnp.sum(bias_heads[...], axis=0)[:, : bias_out_ref.shape[1]]
    wait_all(send_oq, recv_oq, 0, True)
    unpack(recv_oq, dq_ref, o_ref)
    wait_all(send_dkv, recv_dkv, 1, True)
    unpack(recv_dkv, dk_ref, dv_ref)
    wait_all(send_oq, recv_oq, 0, False)
    wait_all(send_dkv, recv_dkv, 1, False)
    wait_all(bias_groups, bias_groups, 2, False, groups)
    wait_all(bias_heads, bias_heads, 3, False)


def local(
    queries, keys, values, out_grad, cluster_perm, tile_ids, tile_counts, hop_class, hop_bias
):
    count = lax.axis_size("seq")
    nodes = cluster_perm.shape[1]
    tiles = nodes // TILE
    columns = queries.shape[2]
    classes, heads = hop_bias.shape
    vmem = pl.BlockSpec(memory_space=pltpu.VMEM)
    smem = pl.BlockSpec(memory_space=pltpu.SMEM)
    bf16, f32 = jnp.bfloat16, jnp.float32
    blocks = (count, TILE, TILE)

    kv, kvt, qg, inverse, pairs = pl.pallas_call(
        functools.partial(inbound_kernel, count),
        out_shape=(
            jax.ShapeDtypeStruct(blocks, bf16),
            jax.ShapeDtypeStruct(blocks, bf16),
            jax.ShapeDtypeStruct(blocks, bf16),
            jax.ShapeDtypeStruct((64, 64), jnp.int32),
            jax.ShapeDtypeStruct((3, TILE), jnp.int32),
        ),
        in_specs=[vmem] * 4 + [smem, vmem] + [smem] * 3,
        out_specs=(vmem, vmem, vmem, vmem, smem),
        scratch_shapes=[
            pltpu.VMEM(blocks, bf16),
            pltpu.VMEM(blocks, bf16),
            pltpu.VMEM(blocks, bf16),
            pltpu.VMEM((nodes, TILE), f32),
            pltpu.VMEM((TILE, TILE), f32),
            pltpu.SemaphoreType.DMA((2,)),
            pltpu.SemaphoreType.DMA((2,)),
        ],
        compiler_params=pltpu.CompilerParams(
            collective_id=0, has_side_effects=True, vmem_limit_bytes=32 << 20
        ),
        name="inbound",
    )(
        queries[0],
        keys[0],
        values[0],
        out_grad[0],
        cluster_perm,
        cluster_perm,
        tile_ids,
        tile_counts,
        hop_class,
    )

    oq, dkv, bias_part = pl.pallas_call(
        functools.partial(attention_kernel, 4),
        out_shape=(
            jax.ShapeDtypeStruct((tiles, TILE, TILE), f32),
            jax.ShapeDtypeStruct((tiles, TILE, TILE), f32),
            jax.ShapeDtypeStruct((classes, TILE), f32),
        ),
        in_specs=[vmem] * 3 + [smem] * 3,
        out_specs=(vmem,) * 3,
        scratch_shapes=[
            pltpu.VMEM((nodes, TILE), f32),
            pltpu.VMEM((TILE, TILE), f32),
            pltpu.VMEM((tiles, 2 * TILE, TILE), bf16),
            pltpu.VMEM((TILE, TILE, TILE), f32),
            pltpu.VMEM((TILE, TILE, TILE), f32),
            pltpu.VMEM((tiles, 8, TILE), f32),
            pltpu.VMEM((tiles, 8, TILE), f32),
            pltpu.VMEM((tiles, 8, TILE), f32),
            pltpu.VMEM((tiles, TILE, TILE), f32),
            pltpu.VMEM((tiles, TILE, TILE), f32),
            pltpu.VMEM((classes, 8, TILE), f32),
        ],
        compiler_params=pltpu.CompilerParams(vmem_limit_bytes=48 << 20),
        name="attention",
    )(kv, kvt, qg, cluster_perm, pairs, hop_bias)

    one_output = jax.ShapeDtypeStruct((TILE, columns), bf16)
    attended, query_grad, key_grad, value_grad, bias_grad = pl.pallas_call(
        functools.partial(outbound_kernel, count),
        out_shape=(one_output,) * 4 + (jax.ShapeDtypeStruct((classes, heads), f32),),
        in_specs=[vmem, vmem, smem, vmem],
        out_specs=(vmem,) * 5,
        scratch_shapes=[
            pltpu.VMEM(blocks, bf16),
            pltpu.VMEM(blocks, bf16),
            pltpu.VMEM(blocks, bf16),
            pltpu.VMEM(blocks, bf16),
            pltpu.VMEM((TILE, TILE), f32),
            pltpu.VMEM((lax.axis_size("dp"), classes, TILE), f32),
            pltpu.VMEM((classes, TILE), f32),
            pltpu.VMEM((count, classes, TILE), f32),
            pltpu.SemaphoreType.DMA((4,)),
            pltpu.SemaphoreType.DMA((4,)),
        ],
        compiler_params=pltpu.CompilerParams(
            collective_id=1, has_side_effects=True, vmem_limit_bytes=32 << 20
        ),
        name="outbound",
    )(oq.reshape(nodes, TILE), dkv.reshape(nodes, TILE), inverse, bias_part)

    return attended[None], query_grad[None], key_grad[None], value_grad[None], bias_grad


def solution(mesh):
    wide = P("dp", "seq", None)
    return jax.shard_map(
        local,
        mesh=mesh,
        in_specs=(
            wide,
            wide,
            wide,
            wide,
            P("dp", None),
            P("dp", None, None),
            P("dp", None),
            P("dp", None, None),
            P(),
        ),
        out_specs=(wide, wide, wide, wide, P()),
        check_vma=False,
    )
```

time: 582 us -> 167 us (0.29)
  local copies, waits for them, and re-layouts: 194 us -> 12.4 us
  Pallas kernels: 0 us -> 152 us
  matrix products: 146 us -> 0 us
  blocking collectives: 103 us -> 0 us
  starting transfers between devices: 68.8 us -> 0 us
  waiting for transfers between devices: 35.9 us -> 0 us
  other arithmetic: 28.1 us -> 0 us
    pallas_call x0 -> x3, Pallas kernels: none -> 152 us  [the longest x1 64.2 us: local(): pl.pallas_call(functools.partial(outbound_kernel, count), out_shape=(one_...]
    dot_general x96 -> x0, matrix products: 146 us -> none  [the longest x8 30.4 us: advance(): jnp.einsum('qst,qsbhe->tbhe', placing, value_part, precision=exact_mode)]
    gather x41 -> x0, local copies, waits for them, and re-layouts: 130 us -> none  [the longest x5 49 us: restore(): return tensor[inverse]]
    psum x1 -> x0, blocking collectives: 103 us -> none  [local(): bias_grad = lax.psum(padded, ('dp', 'seq'))]
    all_to_all x8 -> x0, starting transfers between devices: 68.8 us -> none  [the longest x1 13.7 us: local(): lax.all_to_all(split_heads(values), 'seq', split_axis=1, concat_axis=0, t...]
    all_to_all x8 -> x0, waiting for transfers between devices: 35.9 us -> none  [the longest x1 15.3 us: local(): lax.all_to_all(split_heads(values), 'seq', split_axis=1, concat_axis=0, t...]
    unnamed x45 -> x25, local copies, waits for them, and re-layouts: 32 us -> 12.4 us
    all_to_all x12 -> x0, local copies, waits for them, and re-layouts: 15.6 us -> none  [the longest x2 3.81 us: local(): lax.all_to_all(restore(key_grad), 'seq', split_axis=0, concat_axis=1, til...]
  transfers between devices with their start and end apart: 8 -> 0, of which waited for: 3 -> 0; matrix products, arithmetic and copies ran while one was open for 29% -> 0% of each run, Pallas kernels for 0% -> 0%
where the time goes in v1:
time: 167 us; the launch traced here: 166 us
  Pallas kernels  152 us (91%)
  local copies, waits for them, and re-layouts  12.4 us (7%)
    pallas_call x1, Pallas kernels, local(): pl.pallas_call(functools.partial(outbound_kernel, count), out_shape=(one_...  64.2 us
    pallas_call x1, Pallas kernels, local(): pl.pallas_call(functools.partial(inbound_kernel, count), out_shape=(jax.S...  59.2 us
    pallas_call x1, Pallas kernels, local(): pl.pallas_call(functools.partial(attention_kernel, 4), out_shape=(jax.Sha...  29.1 us
    unnamed x25, local copies, waits for them, and re-layouts  12.4 us

profile of v1, /device:TPU:1, one launch (start us, length us, event | category | flops | bytes accessed | tf_op | source)
XLA Modules:
  0.0 165.6 jit_solution(3983413281598207687)
XLA Ops:
  0.6 0.0 copy-start.6
  0.6 0.0 copy-start.7
  0.7 0.8 copy.14.ids_ref
  1.4 0.8 copy.15.class_ref
  2.2 0.0 copy-start.1
  2.2 1.0 copy-done.1
  3.2 0.0 copy-start.2
  3.2 1.0 copy-done.2
  4.3 0.0 copy-start.3
  4.3 1.0 copy-done.3
  5.3 0.0 copy-start.4
  5.3 1.0 copy-done.4
  6.4 0.0 copy-start.5
  6.4 0.7 copy-done.5
  7.1 0.0 copy-start.8
  7.1 0.7 copy-done.8
  7.7 59.2 %inbound.1 = (bf16[32,128,128]{2,1,0:T(8,128)(2,1)S(1)}, bf16[32,128,128]{2,1,0:T(8,128)(2,1)S(1)}, bf16[32,128,128]{2,1,0:T(8,128)(2,1)S(1)}, s32[64,64]{1,0:T(8,128)S(1)}, s32[3,128]{1,0:T(4,128)S(1)}) custom-call(bf16[128,2048]{1,0:T(8,128)(2,1)S(1)} %bitcast.12, bf16[128,2048]{1,0:T(8,128)(2,1)S(1)} %bitcast.13, bf16[128,2048]{1,0:T(8,128)(2,1)S(1)} %bitcast.14, ...), custom_call_target="tpu_custom_call" | custom-call | tf_op jit(solution)/shard_map/inbound/pallas_call | solution.py:404
  66.9 0.0 copy-done.6
  66.9 0.0 copy-done.7
  66.9 29.1 %attention.1 = (f32[32,128,128]{2,1,0:T(8,128)S(1)}, f32[32,128,128]{2,1,0:T(8,128)}, f32[8,128]{1,0:T(8,128)S(1)}) custom-call(bf16[32,128,128]{2,1,0:T(8,128)(2,1)S(1)} %get-tuple-element.18.kv_ref, bf16[32,128,128]{2,1,0:T(8,128)(2,1)S(1)} %get-tuple-element.19.kvt_ref, bf16[32,128,128]{2,1,0:T(8,128)(2,1)S(1)} %get-tuple-element.20.qg_ref, ...), custom_call_target="tpu_custom_call" | custom-call | tf_op jit(solution)/shard_map/attention/pallas_call | solution.py:440
  96.1 0.0 copy-start
  96.1 1.6 copy-done
  97.7 64.2 %outbound.1 = (bf16[128,2048]{1,0:T(8,128)(2,1)S(1)}, bf16[128,2048]{1,0:T(8,128)(2,1)S(1)}, bf16[128,2048]{1,0:T(8,128)(2,1)S(1)}, bf16[128,2048]{1,0:T(8,128)(2,1)S(1)}, f32[8,32]{1,0:T(8,128)S(1)}) custom-call(f32[4096,128]{1,0:T(8,128)S(1)} %bitcast.10, f32[4096,128]{1,0:T(8,128)S(1)} %bitcast.11, s32[64,64]{1,0:T(8,128)S(1)} %get-tuple-element.24.inverse_ref, ...), custom_call_target="tpu_custom_call" | custom-call | tf_op jit(solution)/shard_map/outbound/pallas_call | solution.py:467
  161.9 0.8 copy.21
  162.7 0.8 copy.22
  163.4 0.8 copy.23
  164.2 0.8 copy.24
  165.0 0.6 copy.25
Async XLA Ops:
  0.6 66.3 %copy-start.6 = (s32[1,4096]{1,0:T(1,128)S(1)}, s32[1,4096]{1,0:T(1,128)}, u32[]{:S(2)}) copy-start(s32[1,4096]{1,0:T(1,128)} %perm_ref.3) | copy-start | bytes 49156
  0.6 66.3 %copy-start.7 = (f32[8,32]{1,0:T(8,128)S(1)}, f32[8,32]{1,0:T(8,128)}, u32[]{:S(2)}) copy-start(f32[8,32]{1,0:T(8,128)} %bias_ref.1) | copy-start | bytes 3076
  2.2 1.0 copy-start.1
  3.2 1.0 copy-start.2
  4.3 1.0 copy-start.3
  5.3 1.0 copy-start.4
  6.4 0.7 copy-start.5
  7.1 0.7 copy-start.8
  96.1 1.6 copy-start

commit v2 on v0

v2 whole, which is shorter than its diff:
```python
import functools
import math

import jax
import jax.numpy as jnp
from jax import lax
from jax.experimental import pallas as pl
from jax.experimental.pallas import tpu as pltpu
from jax.sharding import PartitionSpec as P

MESH = pl.DeviceIdType.MESH
TILE = 128
LOG2E = math.log2(math.e)
NT_DIMS = (((1,), (1,)), ((), ()))
BF16, F32 = jnp.bfloat16, jnp.float32
UNROLL = 32
ABREAST = 4

T_OF, J_OF, P_OF, TQ_OF, JQ_OF, T_LAST, J_LAST = range(7)


def iota(shape, axis):
    return lax.broadcasted_iota(jnp.int32, shape, axis)


def lanes_low():
    return iota((TILE, TILE), 1) < 64


def rolled(block):
    return pltpu.roll(block.astype(F32), 64, 1).astype(BF16)


def folded(block):
    return block.reshape(TILE // 8, 8, TILE)


def gather_rows(source, rows_out, index_of):
    for r in range(TILE):
        rows_out[pl.ds(r, 1), :] = source[pl.ds(index_of(r), 1), :]


def unrolled(count, factor, body):
    def turn(step, carry):
        for u in range(factor):
            body(step * factor + u)
        return carry

    lax.fori_loop(0, count // factor, turn, jnp.int32(0))


def write_lists(head, ids_ref, counts_ref, class_ref, bias_ref, list_ref, pair_bias_ref, hot_ref):
    slots, tiles = ids_ref.shape[1], ids_ref.shape[2]
    flat = tiles * slots
    lane_slot = iota((tiles, flat), 1) % slots
    own = iota((tiles, flat), 1) // slots == iota((tiles, flat), 0)

    diagonal = iota((tiles, tiles), 0) == iota((tiles, tiles), 1)

    def upright(row):
        return jnp.sum(jnp.where(diagonal, row, 0.0), axis=1, keepdims=True)

    def flat_row(table):
        spread = jnp.zeros((tiles, flat), F32)
        for s in range(slots):
            spread = jnp.where(lane_slot == s, upright(table[s : s + 1, :]), spread)
        return jnp.sum(jnp.where(own, spread, 0.0), axis=0, keepdims=True)

    def column(row):
        return jnp.broadcast_to(row, (TILE, flat)).T

    counts = upright(counts_ref[...].astype(F32))
    used = jnp.sum(
        jnp.where(own & (lane_slot.astype(F32) < counts), 1.0, 0.0), axis=0, keepdims=True
    )
    tile_row = flat_row(ids_ref[0].astype(F32))
    class_row = flat_row(class_ref[0].astype(F32))
    used_col, tile_col, class_col = column(used), column(tile_row), column(class_row)
    place = iota((flat, TILE), 0)
    place_wide = place.astype(F32)
    query_col = (place // slots).astype(F32)
    lane = iota((flat, TILE), 1).astype(F32)

    def ranks(key_col, key_row):
        parts = []
        for start in range(0, flat, TILE):
            before = (used_col > 0.5) & (key_col < key_row[:, start : start + TILE])
            parts.append(jnp.sum(jnp.where(before, 1.0, 0.0), axis=0, keepdims=True))
        return column(jnp.concatenate(parts, axis=1))

    place_row = iota((1, flat), 1).astype(F32)
    by_query = ranks(place_wide, place_row)
    by_key = ranks(tile_col * flat + place_wide, tile_row * flat + place_row)

    def pick(rank, values):
        return jnp.sum(
            jnp.where((rank == lane) & (used_col > 0.5), values, 0.0), axis=0, keepdims=True
        )

    def last(values):
        reached = (used_col > 0.5) & (values <= lane)
        return jnp.sum(jnp.where(reached, 1.0, 0.0), axis=0, keepdims=True) - 1.0

    class_of = pick(by_query, class_col)
    rows = (
        pick(by_query, query_col),
        pick(by_query, tile_col),
        pick(by_key, by_query),
        pick(by_key, query_col),
        pick(by_key, tile_col),
        last(query_col),
        last(tile_col),
    )
    table = jnp.concatenate(rows + (jnp.zeros((8 - len(rows), TILE), F32),), axis=0)
    list_ref[...] = jnp.clip(table.astype(jnp.int32), 0, TILE - 1)

    classes, heads = bias_ref.shape
    hot = jnp.where(iota((classes, TILE), 0).astype(F32) == class_of, 1.0, 0.0)
    hot_ref[...] = hot
    own_bias = jnp.sum(
        jnp.where(iota((classes, heads), 1) == head, bias_ref[...], 0.0), axis=1, keepdims=True
    )
    pair_bias = jnp.sum(hot * own_bias, axis=0, keepdims=True) * LOG2E
    pair_bias_ref[...] = jnp.broadcast_to(pair_bias, pair_bias_ref.shape)


def write_inverse(perm_ref, inverse_ref):
    high_total = jnp.zeros((64, 64), F32)
    low_total = jnp.zeros((64, 64), F32)
    width = 1024
    for start in range(0, perm_ref.shape[1], width):
        node = perm_ref[:, pl.ds(start, width)]
        digit = iota((64, width), 0)
        position = iota((64, width), 1) + start
        at_high = lax.shift_right_logical(node, 6) == digit
        at_low = jnp.where((node & 63) == digit, 1.0, 0.0).astype(BF16)
        high_value = lax.shift_right_logical(position, 6).astype(F32)
        low_value = (position & 63).astype(F32)
        high_rows = jnp.where(at_high, high_value, 0.0).astype(BF16)
        low_rows = jnp.where(at_high, low_value, 0.0).astype(BF16)
        high_total += lax.dot_general(high_rows, at_low, NT_DIMS, preferred_element_type=F32)
        low_total += lax.dot_general(low_rows, at_low, NT_DIMS, preferred_element_type=F32)
    found = (high_total * 64.0 + low_total).astype(jnp.int32)
    inverse_ref[...] = jnp.clip(found, 0, perm_ref.shape[1] - 1)


def kernel(
    count,
    groups,
    q_hbm,
    k_hbm,
    v_hbm,
    g_hbm,
    perm,
    lists,
    pair_bias,
    inverse,
    hot,
    o_ref,
    dq_ref,
    dk_ref,
    dv_ref,
    bias_out_ref,
    q_in,
    k_in,
    v_in,
    g_in,
    send_whole,
    land_whole,
    send_half,
    land_half,
    wide,
    rows_0,
    rows_1,
    rows_2,
    rows_3,
    key_query,
    key_t,
    query_t,
    query_low,
    value,
    value_t,
    grad_t,
    grad_low,
    scores,
    grads,
    probs,
    run_tile,
    run_row,
    bias_pairs,
    bias_own,
    bias_groups,
    bias_sum,
    bias_heads,
    local_sem,
    send_sem,
    recv_sem,
):
    me = lax.axis_index("seq")
    group = lax.axis_index("dp")
    tiles = key_query.shape[0]
    pairs = scores.shape[0]
    low = lanes_low()
    low_half = low[:64]
    rows_of = (rows_0, rows_1, rows_2, rows_3)
    run_key = grads
    low_grads = probs

    def peer(step):
        return lax.rem(me + step, count)

    def group_peer(step):
        return lax.rem(group + step, groups)

    def stage(number, source, target):
        return pltpu.make_async_copy(source, target, local_sem.at[number])

    staged = [
        stage(number, source, target)
        for number, (source, target) in enumerate(
            (
                (k_hbm, k_in),
                (q_hbm, q_in),
                (v_hbm, v_in),
                (g_hbm, g_in),
            )
        )
    ]
    for copy in staged:
        copy.start()

    barrier = pltpu.get_barrier_semaphore()

    @pl.loop(1, count)
    def _(step):
        pl.semaphore_signal(barrier, inc=1, device_id=(group, peer(step)), device_id_type=MESH)

    @pl.loop(1, groups)
    def _(step):
        pl.semaphore_signal(barrier, inc=1, device_id=(group_peer(step), me), device_id_type=MESH)

    def remote(src, dst, which, other, other_group):
        return pltpu.make_async_remote_copy(
            src_ref=src,
            dst_ref=dst,
            send_sem=send_sem.at[which],
            recv_sem=recv_sem.at[which],
            device_id=(other_group, other),
            device_id_type=MESH,
        )

    KEY_QUERY, VALUE, GRAD, OUT, VALUE_GRAD, KEY_QUERY_GRAD = range(6)
    buffers = {
        KEY_QUERY: (send_whole.at[0], land_whole.at[0]),
        VALUE: (send_half.at[0], land_half.at[0]),
        GRAD: (send_half.at[1], land_half.at[1]),
        OUT: (send_half.at[2], land_half.at[2]),
        VALUE_GRAD: (send_half.at[3], land_half.at[3]),
        KEY_QUERY_GRAD: (send_whole.at[1], land_whole.at[1]),
    }

    def send_block(which, other):
        out, landing = buffers[which]
        remote(out.at[other], landing.at[me], which, other, group).start()

    def keep_own(which):
        out, landing = buffers[which]
        landing[me] = out[me]

    def all_blocks(which):
        out, landing = buffers[which]
        blocks = pl.ds(0, count - 1)
        return remote(out.at[blocks], landing.at[blocks], which, peer(1), group)

    def send_all(which):
        @pl.loop(1, count)
        def _(step):
            send_block(which, peer(step))

        keep_own(which)

    def columns_of(pair):
        return pl.ds(pl.multiple_of(pair * TILE, TILE), TILE)

    def rows_at(tile):
        return pl.ds(pl.multiple_of(tile * TILE, TILE), TILE)

    def pack(first_ref, second_ref, which):
        out, _ = buffers[which]

        def one(pair):
            columns = columns_of(pair)
            first, second = first_ref[0, :, columns], second_ref[0, :, columns]
            out[2 * pair] = jnp.where(low, first, rolled(second))
            out[2 * pair + 1] = jnp.where(low, rolled(first), second)

        unrolled(count // 2, ABREAST, one)

    def pack_half(source, which):
        out, _ = buffers[which]

        def one(pair):
            columns = columns_of(pair)
            top, bottom = source[0, pl.ds(0, 64), columns], source[0, pl.ds(64, 64), columns]
            out[2 * pair] = jnp.where(low_half, top, rolled(bottom))
            out[2 * pair + 1] = jnp.where(low_half, rolled(top), bottom)

        unrolled(count // 2, ABREAST, one)

    staged[0].wait()
    staged[1].wait()
    pack(k_in, q_in, KEY_QUERY)
    pl.semaphore_wait(barrier, count + groups - 2)
    send_all(KEY_QUERY)
    staged[2].wait()
    pack_half(v_in, VALUE)
    send_all(VALUE)
    staged[3].wait()
    pack_half(g_in, GRAD)
    send_all(GRAD)

    def cluster(use):
        @pl.loop(0, tiles // ABREAST)
        def _(step):
            for u in range(ABREAST):
                base = (step * ABREAST + u) * TILE
                gather_rows(wide, rows_of[u], lambda r, base=base: perm[0, base + r])
            for u in range(ABREAST):
                use(step * ABREAST + u, rows_of[u][...])

    def widen(which):
        landing = buffers[which][1]

        def one(block):
            wide[rows_at(block), :] = landing[block].astype(F32)

        unrolled(count, ABREAST, one)

    def widen_half(which):
        landing = buffers[which][1]

        def one(block):
            both = landing[block].astype(F32)
            wide[rows_at(block), :] = jnp.concatenate([both, pltpu.roll(both, 64, 1)], axis=0)

        unrolled(count, ABREAST, one)

    empty = jnp.zeros((64, TILE), F32)

    def use_key_query(tile, block):
        key_query[tile] = block.astype(BF16)
        turned = block.T
        key_t[tile] = turned[:64].astype(BF16)
        query_t[tile] = jnp.concatenate([turned[64:] * 0.125, empty], axis=0).astype(BF16)
        query_low[tile] = pltpu.roll(jnp.where(low, 0.0, block * 0.125), 64, 1).astype(BF16)

    all_blocks(KEY_QUERY).wait_recv()
    widen(KEY_QUERY)
    cluster(use_key_query)

    def first_of(row, p):
        return (p == 0) | (lists[row, p] != lists[row, jnp.maximum(p - 1, 0)])

    def over_pairs(start, body):
        def chunk(step, carry):
            for u in range(UNROLL):
                carry = body(step * UNROLL + u, carry)
            return carry

        lax.fori_loop(0, pairs // UNROLL, chunk, start)

    none = jnp.zeros((8, TILE), F32)

    def score_pair(p, peak):
        t, j = lists[T_OF, p], lists[J_OF, p]
        product = jnp.dot(key_query[j], query_t[t], preferred_element_type=F32)
        score = product * LOG2E + pair_bias[0, p]
        scores[p] = score
        before = jnp.where(first_of(T_OF, p), -jnp.inf, peak)
        peak = jnp.maximum(before, jnp.max(folded(score), axis=0))
        run_row[p] = peak
        return peak

    over_pairs(none, score_pair)
    run_row[...] = jnp.broadcast_to(jnp.max(run_row[...], axis=1, keepdims=True), run_row.shape)

    def power_pair(p, total):
        end = lists[T_LAST, lists[T_OF, p]]
        power = jnp.exp2(folded(scores[p]) - run_row[end][None])
        scores[p] = power.reshape(TILE, TILE)
        total = jnp.where(first_of(T_OF, p), 0.0, total) + jnp.sum(power, axis=0)
        bias_pairs[p] = total
        return total

    over_pairs(none, power_pair)
    bias_pairs[...] = jnp.broadcast_to(
        1.0 / jnp.sum(bias_pairs[...], axis=1, keepdims=True), bias_pairs.shape
    )

    def prob_pair(p, carry):
        end = lists[T_LAST, lists[T_OF, p]]
        prob = (folded(scores[p]) * bias_pairs[end][None]).reshape(TILE, TILE)
        scores[p] = prob
        probs[p] = prob.astype(BF16)
        return carry

    over_pairs(jnp.int32(0), prob_pair)

    def by_query_tile(left, right):
        def body(p, total):
            part = jnp.dot(left[lists[J_OF, p]], right[p], preferred_element_type=F32)
            total = jnp.where(first_of(T_OF, p), 0.0, total) + part
            run_tile[p] = total
            return total

        over_pairs(empty, body)

    def by_key_tile(left, right):
        def body(q, total):
            part = jnp.dot(
                left[lists[P_OF, q]], right[lists[TQ_OF, q]], preferred_element_type=F32
            )
            total = jnp.where(first_of(JQ_OF, q), 0.0, total) + part
            run_key[q] = total
            return total

        over_pairs(jnp.zeros((TILE, TILE), F32), body)

    def send_wide(which, half):
        out, _ = buffers[which]

        @pl.loop(0, count // ABREAST)
        def _(turn):
            for u in range(ABREAST):
                other = peer(turn * ABREAST + u + 1)
                gather_rows(
                    wide,
                    rows_of[u],
                    lambda r, other=other: inverse[2 * other + r // 64, r % 64],
                )
            for u in range(ABREAST):
                other = peer(turn * ABREAST + u + 1)
                block = rows_of[u][...]
                if half:
                    block = jnp.where(low_half, block[:64], pltpu.roll(block[64:], 64, 1))
                out[other] = block.astype(BF16)
            for u in range(ABREAST):
                step = turn * ABREAST + u + 1
                if u < ABREAST - 1:
                    send_block(which, peer(step))
                else:

                    @pl.when(step < count)
                    def _():
                        send_block(which, peer(step))

        keep_own(which)

    def use_value(tile, block):
        value[tile] = block.astype(BF16)
        value_t[tile] = block.T[:64].astype(BF16)

    all_blocks(VALUE).wait_recv()
    widen_half(VALUE)
    cluster(use_value)
    by_query_tile(value_t, probs)

    def turn_out(tile):
        of_query = run_tile[lists[T_LAST, tile]]
        wide[rows_at(tile), :] = jnp.concatenate([of_query, empty], axis=0).T

    unrolled(tiles, ABREAST, turn_out)
    send_wide(OUT, True)

    def use_grad(tile, block):
        grad_low[tile] = jnp.where(low, block, 0.0).astype(BF16)
        grad_t[tile] = jnp.concatenate([block.T[:64], empty], axis=0).astype(BF16)

    all_blocks(GRAD).wait_recv()
    widen_half(GRAD)
    cluster(use_grad)
    by_key_tile(probs, grad_low)

    def place_value_grad(tile):
        wide[rows_at(tile), :] = run_key[lists[J_LAST, tile]]

    unrolled(tiles, ABREAST, place_value_grad)
    send_wide(VALUE_GRAD, True)

    def prob_grad_pair(p, dots):
        t, j = lists[T_OF, p], lists[J_OF, p]
        product = jnp.dot(value[j], grad_t[t], preferred_element_type=F32)
        grads[p] = product
        dots = jnp.where(first_of(T_OF, p), 0.0, dots) + jnp.sum(
            folded(scores[p]) * folded(product), axis=0
        )
        run_row[p] = dots
        return dots

    over_pairs(none, prob_grad_pair)
    run_row[...] = jnp.broadcast_to(jnp.sum(run_row[...], axis=1, keepdims=True), run_row.shape)

    def score_grad_pair(p, carry):
        end = lists[T_LAST, lists[T_OF, p]]
        grad = folded(scores[p]) * (folded(grads[p]) - run_row[end][None])
        bias_pairs[p] = jnp.sum(grad, axis=0)
        low_grads[p] = grad.reshape(TILE, TILE).astype(BF16)
        return carry

    over_pairs(jnp.int32(0), score_grad_pair)
    by_query_tile(key_t, low_grads)
    by_key_tile(low_grads, query_low)

    def place_key_query_grad(tile):
        of_query = run_tile[lists[T_LAST, tile]] * 0.125
        of_key = run_key[lists[J_LAST, tile]]
        wide[rows_at(tile), :] = jnp.concatenate([empty, of_query], axis=0).T + of_key

    unrolled(tiles, ABREAST, place_key_query_grad)

    left = jnp.sum(bias_pairs[...], axis=1)
    class_sums = jnp.zeros((hot.shape[0], TILE), F32)
    hot_low = hot[...].astype(BF16)
    for _ in range(3):
        part = left.astype(BF16)
        class_sums += jnp.dot(hot_low, part, preferred_element_type=F32)
        left = left - part.astype(F32)
    own_column = iota(bias_own.shape, 1) == me
    bias_own[...] = jnp.where(own_column, jnp.sum(class_sums, axis=1, keepdims=True), 0.0)

    @pl.loop(1, groups)
    def _(step):
        remote(bias_own, bias_groups.at[group], 6, me, group_peer(step)).start()

    bias_groups[group] = bias_own[...]
    send_wide(KEY_QUERY_GRAD, False)

    own_groups = pl.ds(0, groups - 1)
    group_copies = remote(
        bias_groups.at[own_groups], bias_groups.at[own_groups], 6, me, group_peer(1)
    )
    group_copies.wait_recv()
    bias_sum[...] = jnp.sum(bias_groups[...], axis=0)

    @pl.loop(1, count)
    def _(step):
        remote(bias_sum, bias_heads.at[me], 7, peer(step), group).start()

    bias_heads[me] = bias_sum[...]

    def unpack_half(which, target):
        landing = buffers[which][1]

        def one(pair):
            even, odd = landing[2 * pair], landing[2 * pair + 1]
            target[pl.ds(0, 64), columns_of(pair)] = jnp.where(low_half, even, rolled(odd))
            target[pl.ds(64, 64), columns_of(pair)] = jnp.where(low_half, rolled(even), odd)

        unrolled(count // 2, ABREAST, one)

    def unpack(which, first_ref, second_ref):
        landing = buffers[which][1]

        def one(pair):
            even, odd = landing[2 * pair], landing[2 * pair + 1]
            first_ref[:, columns_of(pair)] = jnp.where(low, even, rolled(odd))
            second_ref[:, columns_of(pair)] = jnp.where(low, rolled(even), odd)

        unrolled(count // 2, ABREAST, one)

    all_blocks(OUT).wait_recv()
    unpack_half(OUT, o_ref)
    all_blocks(VALUE_GRAD).wait_recv()
    unpack_half(VALUE_GRAD, dv_ref)
    own_heads = pl.ds(0, count - 1)
    head_copies = remote(bias_heads.at[own_heads], bias_heads.at[own_heads], 7, peer(1), group)
    head_copies.wait_recv()
    bias_out_ref[...] = jnp.sum(bias_heads[...], axis=0)[:, : bias_out_ref.shape[1]]
    for which in (KEY_QUERY, VALUE, GRAD, OUT, VALUE_GRAD):
        all_blocks(which).wait_send()
    group_copies.wait_send()
    head_copies.wait_send()
    all_blocks(KEY_QUERY_GRAD).wait_recv()
    unpack(KEY_QUERY_GRAD, dk_ref, dq_ref)
    all_blocks(KEY_QUERY_GRAD).wait_send()


def plan(perm_ref, ids_ref, counts_ref, class_ref, bias_ref, list_ref, pair_bias_ref, inverse_ref, hot_ref):
    head = lax.axis_index("seq")
    write_lists(head, ids_ref, counts_ref, class_ref, bias_ref, list_ref, pair_bias_ref, hot_ref)
    write_inverse(perm_ref, inverse_ref)


def write_out(*refs):
    sources, targets, sems = refs[:5], refs[5:10], refs[10]
    copies = []
    for number, (source, target) in enumerate(zip(sources, targets)):
        place = target if number == 4 else target.at[0]
        copies.append(pltpu.make_async_copy(source, place, sems.at[number]))
    for copy in copies:
        copy.start()
    for copy in copies:
        copy.wait()


def local(
    queries, keys, values, out_grad, cluster_perm, tile_ids, tile_counts, hop_class, hop_bias
):
    count, groups = lax.axis_size("seq"), lax.axis_size("dp")
    nodes = cluster_perm.shape[1]
    tiles = nodes // TILE
    columns = queries.shape[2]
    classes, heads = hop_bias.shape
    pairs = TILE
    i32 = jnp.int32
    any_space = pl.BlockSpec(memory_space=pl.ANY)
    vmem = pl.BlockSpec(memory_space=pltpu.VMEM)
    smem = pl.BlockSpec(memory_space=pltpu.SMEM)
    one_output = jax.ShapeDtypeStruct((TILE, columns), BF16)
    bias_output = jax.ShapeDtypeStruct((classes, heads), F32)
    tile_blocks = pltpu.VMEM((tiles, TILE, TILE), BF16)
    half_blocks = pltpu.VMEM((tiles, 64, TILE), BF16)

    lists, pair_bias, inverse, hot = pl.pallas_call(
        plan,
        out_shape=(
            jax.ShapeDtypeStruct((8, TILE), i32),
            jax.ShapeDtypeStruct((8, TILE), F32),
            jax.ShapeDtypeStruct((64, 64), i32),
            jax.ShapeDtypeStruct((classes, TILE), F32),
        ),
        in_specs=[vmem] * 5,
        out_specs=(vmem,) * 4,
        compiler_params=pltpu.CompilerParams(vmem_limit_bytes=4 << 20),
        name="plan",
    )(
        cluster_perm,
        jnp.swapaxes(tile_ids, 1, 2),
        tile_counts,
        jnp.swapaxes(hop_class, 1, 2),
        hop_bias,
    )

    results = pl.pallas_call(
        functools.partial(kernel, count, groups),
        out_shape=(one_output,) * 4 + (bias_output,),
        in_specs=[any_space] * 4 + [smem] * 4 + [vmem],
        out_specs=(vmem,) * 5,
        scratch_shapes=[pltpu.VMEM((1, TILE, columns), BF16)] * 4
        + [
            pltpu.VMEM((2, count, TILE, TILE), BF16),
            pltpu.VMEM((2, count, TILE, TILE), BF16),
            pltpu.VMEM((4, count, 64, TILE), BF16),
            pltpu.VMEM((4, count, 64, TILE), BF16),
            pltpu.VMEM((nodes, TILE), F32),
        ]
        + [pltpu.VMEM((TILE, TILE), F32)] * 4
        + [
            tile_blocks,
            half_blocks,
            tile_blocks,
            tile_blocks,
            tile_blocks,
            half_blocks,
            tile_blocks,
            tile_blocks,
            pltpu.VMEM((pairs, TILE, TILE), F32),
            pltpu.VMEM((pairs, TILE, TILE), F32),
            pltpu.VMEM((pairs, TILE, TILE), BF16),
            pltpu.VMEM((pairs, 64, TILE), F32),
            pltpu.VMEM((pairs, 8, TILE), F32),
            pltpu.VMEM((pairs, 8, TILE), F32),
            pltpu.VMEM((classes, TILE), F32),
            pltpu.VMEM((groups, classes, TILE), F32),
            pltpu.VMEM((classes, TILE), F32),
            pltpu.VMEM((count, classes, TILE), F32),
            pltpu.SemaphoreType.DMA((4,)),
            pltpu.SemaphoreType.DMA((8,)),
            pltpu.SemaphoreType.DMA((8,)),
        ],
        compiler_params=pltpu.CompilerParams(
            collective_id=0, has_side_effects=True, vmem_limit_bytes=51 << 20
        ),
        name="graph_attention",
    )(
        queries,
        keys,
        values,
        out_grad,
        cluster_perm,
        lists,
        pair_bias,
        inverse,
        hot,
    )

    whole_output = jax.ShapeDtypeStruct((1, TILE, columns), BF16)
    return pl.pallas_call(
        write_out,
        out_shape=(whole_output,) * 4 + (bias_output,),
        in_specs=[vmem] * 5,
        out_specs=(any_space,) * 5,
        scratch_shapes=[pltpu.SemaphoreType.DMA((5,))],
        compiler_params=pltpu.CompilerParams(vmem_limit_bytes=1 << 20),
        name="write_out",
    )(*results)


def solution(mesh):
    wide = P("dp", "seq", None)
    return jax.shard_map(
        local,
        mesh=mesh,
        in_specs=(
            wide,
            wide,
            wide,
            wide,
            P("dp", None),
            P("dp", None, None),
            P("dp", None),
            P("dp", None, None),
            P(),
        ),
        out_specs=(wide, wide, wide, wide, P()),
        check_vma=False,
    )
```

time: 582 us -> 122 us (0.21)
  local copies, waits for them, and re-layouts: 194 us -> 4.6 us
  matrix products: 146 us -> 0 us
  Pallas kernels: 0 us -> 116 us
  blocking collectives: 103 us -> 0 us
  starting transfers between devices: 68.8 us -> 0 us
  waiting for transfers between devices: 35.9 us -> 0 us
  other arithmetic: 28.1 us -> 0 us
    dot_general x96 -> x0, matrix products: 146 us -> none  [the longest x8 30.4 us: advance(): jnp.einsum('qst,qsbhe->tbhe', placing, value_part, precision=exact_mode)]
    gather x41 -> x0, local copies, waits for them, and re-layouts: 130 us -> none  [the longest x5 49 us: restore(): return tensor[inverse]]
    pallas_call x0 -> x3, Pallas kernels: none -> 116 us  [the longest x1 115 us: local(): pl.pallas_call(functools.partial(kernel, count, groups), out_shape=(one_o...]
    psum x1 -> x0, blocking collectives: 103 us -> none  [local(): bias_grad = lax.psum(padded, ('dp', 'seq'))]
    all_to_all x8 -> x0, starting transfers between devices: 68.8 us -> none  [the longest x1 13.7 us: local(): lax.all_to_all(split_heads(values), 'seq', split_axis=1, concat_axis=0, t...]
    all_to_all x8 -> x0, waiting for transfers between devices: 35.9 us -> none  [the longest x1 15.3 us: local(): lax.all_to_all(split_heads(values), 'seq', split_axis=1, concat_axis=0, t...]
    unnamed x45 -> x14, local copies, waits for them, and re-layouts: 32 us -> 4.6 us
    all_to_all x12 -> x0, local copies, waits for them, and re-layouts: 15.6 us -> none  [the longest x2 3.81 us: local(): lax.all_to_all(restore(key_grad), 'seq', split_axis=0, concat_axis=1, til...]
  transfers between devices with their start and end apart: 8 -> 0, of which waited for: 3 -> 0; matrix products, arithmetic and copies ran while one was open for 29% -> 0% of each run, Pallas kernels for 0% -> 0%
where the time goes in v2:
time: 122 us
  Pallas kernels  116 us (95%)
  local copies, waits for them, and re-layouts  4.6 us (4%)
    pallas_call x1, Pallas kernels, local(): pl.pallas_call(functools.partial(kernel, count, groups), out_shape=(one_o...  115 us
    unnamed x14, local copies, waits for them, and re-layouts  4.6 us

profile of v2, /device:TPU:1, one launch (start us, length us, event | category | flops | bytes accessed | tf_op | source)
XLA Modules:
  0.0 121.8 jit_solution(18134898335068007454)
XLA Ops:
  0.6 0.0 copy-start.6
  0.6 0.6 copy-done.6
  1.3 0.0 copy-start.1
  1.3 0.7 copy-done.1
  2.0 0.0 copy-start.3
  2.0 0.7 copy-done.3
  2.7 0.0 copy-start.4
  2.7 0.7 copy-done.4
  3.4 0.0 copy-start.5
  3.4 0.7 copy-done.5
  4.1 0.0 copy-start.2
  4.1 0.6 plan.1
  4.6 0.1 copy-done.2
  4.8 0.0 copy-start
  4.8 1.0 copy-done
  5.8 114.6 %graph_attention.1 = (bf16[128,2048]{1,0:T(8,128)(2,1)S(1)}, bf16[128,2048]{1,0:T(8,128)(2,1)S(1)}, bf16[128,2048]{1,0:T(8,128)(2,1)S(1)}, bf16[128,2048]{1,0:T(8,128)(2,1)S(1)}, f32[8,32]{1,0:T(8,128)S(1)}) custom-call(bf16[1,128,2048]{2,1,0:T(8,128)(2,1)S(1)} %copy-done, bf16[1,128,2048]{2,1,0:T(8,128)(2,1)} %k_hbm.1, bf16[1,128,2048]{2,1,0:T(8,128)(2,1)} %v_hbm.1, ...), custom_call_target="tpu_custom_call" | custom-call | tf_op jit(solution)/shard_map/graph_attention/pallas_call | solution.py:644
  120.4 1.4 %write_out.1 = (bf16[1,128,2048]{2,1,0:T(8,128)(2,1)}, bf16[1,128,2048]{2,1,0:T(8,128)(2,1)}, bf16[1,128,2048]{2,1,0:T(8,128)(2,1)}, bf16[1,128,2048]{2,1,0:T(8,128)(2,1)}, f32[8,32]{1,0:T(8,128)}) custom-call(bf16[128,2048]{1,0:T(8,128)(2,1)S(1)} %get-tuple-element.18.refs_0_, bf16[128,2048]{1,0:T(8,128)(2,1)S(1)} %get-tuple-element.19.refs_1_, ...), custom_call_target="tpu_custom_call" | custom-call | tf_op jit(solution)/shard_map/write_out/pallas_call | solution.py:698
Async XLA Ops:
  0.6 0.7 copy-start.6
  1.3 0.7 copy-start.1
  2.0 0.7 copy-start.3
  2.7 0.7 copy-start.4
  3.4 0.7 copy-start.5
  4.1 0.7 copy-start.2
  4.8 1.0 copy-start

commit v3 on v2

--- a/solution.py
+++ b/solution.py
@@ -151,11 +151,11 @@
     k_hbm,
     v_hbm,
     g_hbm,
-    perm,
-    lists,
-    pair_bias,
-    inverse,
-    hot,
+    perm_hbm,
+    lists_hbm,
+    pair_bias_hbm,
+    inverse_hbm,
+    hot_hbm,
     o_ref,
     dq_ref,
     dk_ref,
@@ -165,6 +165,11 @@
     k_in,
     v_in,
     g_in,
+    perm,
+    lists,
+    pair_bias,
+    inverse,
+    hot,
     send_whole,
     land_whole,
     send_half,
@@ -223,6 +228,11 @@
                 (q_hbm, q_in),
                 (v_hbm, v_in),
                 (g_hbm, g_in),
+                (perm_hbm, perm),
+                (lists_hbm, lists),
+                (pair_bias_hbm, pair_bias),
+                (inverse_hbm, inverse),
+                (hot_hbm, hot),
             )
         )
     ]
@@ -318,6 +328,8 @@
     staged[3].wait()
     pack_half(g_in, GRAD)
     send_all(GRAD)
+    for copy in staged[4:]:
+        copy.wait()
 
     def cluster(use):
         @pl.loop(0, tiles // ABREAST)
@@ -615,7 +627,6 @@
     i32 = jnp.int32
     any_space = pl.BlockSpec(memory_space=pl.ANY)
     vmem = pl.BlockSpec(memory_space=pltpu.VMEM)
-    smem = pl.BlockSpec(memory_space=pltpu.SMEM)
     one_output = jax.ShapeDtypeStruct((TILE, columns), BF16)
     bias_output = jax.ShapeDtypeStruct((classes, heads), F32)
     tile_blocks = pltpu.VMEM((tiles, TILE, TILE), BF16)
@@ -644,10 +655,15 @@
     results = pl.pallas_call(
         functools.partial(kernel, count, groups),
         out_shape=(one_output,) * 4 + (bias_output,),
-        in_specs=[any_space] * 4 + [smem] * 4 + [vmem],
+        in_specs=[any_space] * 9,
         out_specs=(vmem,) * 5,
         scratch_shapes=[pltpu.VMEM((1, TILE, columns), BF16)] * 4
         + [
+            pltpu.SMEM((1, nodes), i32),
+            pltpu.SMEM((8, TILE), i32),
+            pltpu.SMEM((8, TILE), F32),
+            pltpu.SMEM((64, 64), i32),
+            pltpu.VMEM((classes, TILE), F32),
             pltpu.VMEM((2, count, TILE, TILE), BF16),
             pltpu.VMEM((2, count, TILE, TILE), BF16),
             pltpu.VMEM((4, count, 64, TILE), BF16),
@@ -674,12 +690,12 @@
             pltpu.VMEM((groups, classes, TILE), F32),
             pltpu.VMEM((classes, TILE), F32),
             pltpu.VMEM((count, classes, TILE), F32),
-            pltpu.SemaphoreType.DMA((4,)),
+            pltpu.SemaphoreType.DMA((9,)),
             pltpu.SemaphoreType.DMA((8,)),
             pltpu.SemaphoreType.DMA((8,)),
         ],
         compiler_params=pltpu.CompilerParams(
-            collective_id=0, has_side_effects=True, vmem_limit_bytes=51 << 20
+            collective_id=0, has_side_effects=True, vmem_limit_bytes=103 << 19
         ),
         name="graph_attention",
     )(

time: 122 us -> 120 us (0.984)
    pallas_call x1, Pallas kernels: 115 us -> 113 us  [local(): pl.pallas_call(functools.partial(kernel, count, groups), out_shape=(one_o...]
    unnamed x14 -> x12, local copies, waits for them, and re-layouts: 4.6 us -> 3.56 us
where the time goes in v3:
time: 120 us; the launch traced here: 119 us
  Pallas kernels  115 us (96%)
  local copies, waits for them, and re-layouts  3.56 us (3%)
    pallas_call x1, Pallas kernels, local(): pl.pallas_call(functools.partial(kernel, count, groups), out_shape=(one_o...  113 us
    unnamed x12, local copies, waits for them, and re-layouts  3.56 us

profile of v3, /device:TPU:1, one launch (start us, length us, event | category | flops | bytes accessed | tf_op | source)
XLA Modules:
  0.0 119.4 jit_solution(9210936173701817927)
XLA Ops:
  0.6 0.0 copy-start.5
  0.6 0.6 copy-done.5
  1.3 0.0 copy-start
  1.3 0.7 copy-done
  2.0 0.0 copy-start.2
  2.0 0.7 copy-done.2
  2.7 0.0 copy-start.3
  2.7 0.7 copy-done.3
  3.4 0.0 copy-start.4
  3.4 0.7 copy-done.4
  4.1 0.0 copy-start.1
  4.1 0.6 plan.1
  4.6 0.1 copy-done.1
  4.8 113.2 %graph_attention.1 = (bf16[128,2048]{1,0:T(8,128)(2,1)S(1)}, bf16[128,2048]{1,0:T(8,128)(2,1)S(1)}, bf16[128,2048]{1,0:T(8,128)(2,1)S(1)}, bf16[128,2048]{1,0:T(8,128)(2,1)S(1)}, f32[8,32]{1,0:T(8,128)S(1)}) custom-call(bf16[1,128,2048]{2,1,0:T(8,128)(2,1)} %q_hbm.1, bf16[1,128,2048]{2,1,0:T(8,128)(2,1)} %k_hbm.1, bf16[1,128,2048]{2,1,0:T(8,128)(2,1)} %v_hbm.1, ...), custom_call_target="tpu_custom_call" | custom-call | tf_op jit(solution)/shard_map/graph_attention/pallas_call | solution.py:655
  118.0 1.4 %write_out.1 = (bf16[1,128,2048]{2,1,0:T(8,128)(2,1)}, bf16[1,128,2048]{2,1,0:T(8,128)(2,1)}, bf16[1,128,2048]{2,1,0:T(8,128)(2,1)}, bf16[1,128,2048]{2,1,0:T(8,128)(2,1)}, f32[8,32]{1,0:T(8,128)}) custom-call(bf16[128,2048]{1,0:T(8,128)(2,1)S(1)} %get-tuple-element.18.refs_0_, bf16[128,2048]{1,0:T(8,128)(2,1)S(1)} %get-tuple-element.19.refs_1_, ...), custom_call_target="tpu_custom_call" | custom-call | tf_op jit(solution)/shard_map/write_out/pallas_call | solution.py:714
Async XLA Ops:
  0.6 0.7 copy-start.5
  1.3 0.7 copy-start
  2.0 0.7 copy-start.2
  2.7 0.7 copy-start.3
  3.4 0.7 copy-start.4
  4.1 0.7 copy-start.1

commit v4 on v3

--- a/solution.py
+++ b/solution.py
@@ -16,7 +16,7 @@
 UNROLL = 32
 ABREAST = 4
 
-T_OF, J_OF, P_OF, TQ_OF, JQ_OF, T_LAST, J_LAST = range(7)
+T_OF, J_OF, P_OF, TQ_OF, JQ_OF, T_LAST, J_LAST, C_OF = range(8)
 
 
 def iota(shape, axis):
@@ -49,7 +49,7 @@
     lax.fori_loop(0, count // factor, turn, jnp.int32(0))
 
 
-def write_lists(head, ids_ref, counts_ref, class_ref, bias_ref, list_ref, pair_bias_ref, hot_ref):
+def write_lists(ids_ref, counts_ref, class_ref, list_ref, hot_ref):
     slots, tiles = ids_ref.shape[1], ids_ref.shape[2]
     flat = tiles * slots
     lane_slot = iota((tiles, flat), 1) % slots
@@ -110,18 +110,12 @@
         pick(by_key, tile_col),
         last(query_col),
         last(tile_col),
+        class_of,
     )
-    table = jnp.concatenate(rows + (jnp.zeros((8 - len(rows), TILE), F32),), axis=0)
+    table = jnp.concatenate(rows, axis=0)
     list_ref[...] = jnp.clip(table.astype(jnp.int32), 0, TILE - 1)
 
-    classes, heads = bias_ref.shape
-    hot = jnp.where(iota((classes, TILE), 0).astype(F32) == class_of, 1.0, 0.0)
-    hot_ref[...] = hot
-    own_bias = jnp.sum(
-        jnp.where(iota((classes, heads), 1) == head, bias_ref[...], 0.0), axis=1, keepdims=True
-    )
-    pair_bias = jnp.sum(hot * own_bias, axis=0, keepdims=True) * LOG2E
-    pair_bias_ref[...] = jnp.broadcast_to(pair_bias, pair_bias_ref.shape)
+    hot_ref[...] = jnp.where(iota(hot_ref.shape, 0).astype(F32) == class_of, 1.0, 0.0)
 
 
 def write_inverse(perm_ref, inverse_ref):
@@ -153,7 +147,7 @@
     g_hbm,
     perm_hbm,
     lists_hbm,
-    pair_bias_hbm,
+    bias_hbm,
     inverse_hbm,
     hot_hbm,
     o_ref,
@@ -167,7 +161,7 @@
     g_in,
     perm,
     lists,
-    pair_bias,
+    bias,
     inverse,
     hot,
     send_whole,
@@ -230,7 +224,7 @@
                 (g_hbm, g_in),
                 (perm_hbm, perm),
                 (lists_hbm, lists),
-                (pair_bias_hbm, pair_bias),
+                (bias_hbm, bias),
                 (inverse_hbm, inverse),
                 (hot_hbm, hot),
             )
@@ -386,7 +380,7 @@
     def score_pair(p, peak):
         t, j = lists[T_OF, p], lists[J_OF, p]
         product = jnp.dot(key_query[j], query_t[t], preferred_element_type=F32)
-        score = product * LOG2E + pair_bias[0, p]
+        score = product * LOG2E + bias[lists[C_OF, p], me] * LOG2E
         scores[p] = score
         before = jnp.where(first_of(T_OF, p), -jnp.inf, peak)
         peak = jnp.maximum(before, jnp.max(folded(score), axis=0))
@@ -597,9 +591,8 @@
     all_blocks(KEY_QUERY_GRAD).wait_send()
 
 
-def plan(perm_ref, ids_ref, counts_ref, class_ref, bias_ref, list_ref, pair_bias_ref, inverse_ref, hot_ref):
-    head = lax.axis_index("seq")
-    write_lists(head, ids_ref, counts_ref, class_ref, bias_ref, list_ref, pair_bias_ref, hot_ref)
+def plan(perm_ref, ids_ref, counts_ref, class_ref, list_ref, inverse_ref, hot_ref):
+    write_lists(ids_ref, counts_ref, class_ref, list_ref, hot_ref)
     write_inverse(perm_ref, inverse_ref)
 
 
@@ -632,16 +625,15 @@
     tile_blocks = pltpu.VMEM((tiles, TILE, TILE), BF16)
     half_blocks = pltpu.VMEM((tiles, 64, TILE), BF16)
 
-    lists, pair_bias, inverse, hot = pl.pallas_call(
+    lists, inverse, hot = pl.pallas_call(
         plan,
         out_shape=(
             jax.ShapeDtypeStruct((8, TILE), i32),
-            jax.ShapeDtypeStruct((8, TILE), F32),
             jax.ShapeDtypeStruct((64, 64), i32),
             jax.ShapeDtypeStruct((classes, TILE), F32),
         ),
-        in_specs=[vmem] * 5,
-        out_specs=(vmem,) * 4,
+        in_specs=[vmem] * 4,
+        out_specs=(vmem,) * 3,
         compiler_params=pltpu.CompilerParams(vmem_limit_bytes=4 << 20),
         name="plan",
     )(
@@ -649,7 +641,6 @@
         jnp.swapaxes(tile_ids, 1, 2),
         tile_counts,
         jnp.swapaxes(hop_class, 1, 2),
-        hop_bias,
     )
 
     results = pl.pallas_call(
@@ -661,7 +652,7 @@
         + [
             pltpu.SMEM((1, nodes), i32),
             pltpu.SMEM((8, TILE), i32),
-            pltpu.SMEM((8, TILE), F32),
+            pltpu.SMEM(hop_bias.shape, F32),
             pltpu.SMEM((64, 64), i32),
             pltpu.VMEM((classes, TILE), F32),
             pltpu.VMEM((2, count, TILE, TILE), BF16),
@@ -705,7 +696,7 @@
         out_grad,
         cluster_perm,
         lists,
-        pair_bias,
+        hop_bias,
         inverse,
         hot,
     )

time: 120 us -> 120 us (level)
  no operation moved by 1% of the time
where the time goes in v4:
time: 120 us; the launch traced here: 119 us
  Pallas kernels  115 us (96%)
  local copies, waits for them, and re-layouts  3.42 us (3%)
    pallas_call x1, Pallas kernels, local(): pl.pallas_call(functools.partial(kernel, count, groups), out_shape=(one_o...  113 us
    unnamed x12, local copies, waits for them, and re-layouts  3.42 us

profile of v4, /device:TPU:1, one launch (start us, length us, event | category | flops | bytes accessed | tf_op | source)
XLA Modules:
  0.0 119.2 jit_solution(17642028562360356345)
XLA Ops:
  0.6 0.0 copy-start.5
  0.6 0.6 copy-done.5
  1.3 0.0 copy-start
  1.3 0.7 copy-done
  2.0 0.0 copy-start.3
  2.0 0.7 copy-done.3
  2.7 0.0 copy-start.4
  2.7 0.7 copy-done.4
  3.4 0.0 copy-start.1
  3.4 0.6 plan.1
  4.0 0.0 copy-start.2
  4.0 0.1 copy-done.1
  4.1 0.6 copy-done.2
  4.7 113.2 %graph_attention.1 = (bf16[128,2048]{1,0:T(8,128)(2,1)S(1)}, bf16[128,2048]{1,0:T(8,128)(2,1)S(1)}, bf16[128,2048]{1,0:T(8,128)(2,1)S(1)}, bf16[128,2048]{1,0:T(8,128)(2,1)S(1)}, f32[8,32]{1,0:T(8,128)S(1)}) custom-call(bf16[1,128,2048]{2,1,0:T(8,128)(2,1)} %q_hbm.1, bf16[1,128,2048]{2,1,0:T(8,128)(2,1)} %k_hbm.1, bf16[1,128,2048]{2,1,0:T(8,128)(2,1)} %v_hbm.1, ...), custom_call_target="tpu_custom_call" | custom-call | tf_op jit(solution)/shard_map/graph_attention/pallas_call | solution.py:646
  117.9 1.4 %write_out.1 = (bf16[1,128,2048]{2,1,0:T(8,128)(2,1)}, bf16[1,128,2048]{2,1,0:T(8,128)(2,1)}, bf16[1,128,2048]{2,1,0:T(8,128)(2,1)}, bf16[1,128,2048]{2,1,0:T(8,128)(2,1)}, f32[8,32]{1,0:T(8,128)}) custom-call(bf16[128,2048]{1,0:T(8,128)(2,1)S(1)} %get-tuple-element.16.refs_0_, bf16[128,2048]{1,0:T(8,128)(2,1)S(1)} %get-tuple-element.17.refs_1_, ...), custom_call_target="tpu_custom_call" | custom-call | tf_op jit(solution)/shard_map/write_out/pallas_call | solution.py:705
Async XLA Ops:
  0.6 0.7 copy-start.5
  1.3 0.7 copy-start
  2.0 0.7 copy-start.3
  2.7 0.7 copy-start.4
  3.4 0.7 copy-start.1
  4.0 0.7 copy-start.2
